TPU v7x, 256 devices: a whole 4x4x8 slice. The times are simulated.
256 devices in a mesh: row: 8 (over z), col: 32 (over y, x, core).
Axes of the slice: x: 4, y: 4, z: 8, core: 2. Of those that a mesh axis runs over, the one named last changes fastest.
Arguments:
- pair_act: bfloat16 [768, 768, 128], P('row', 'col'), may hold values from -6 to 6
- pair_gain: float32 [128], replicated, may hold values from 0.25 to 1.75
- left_proj: bfloat16 [128, 256], replicated, may hold values from -0.5 to 0.5
- right_proj: bfloat16 [128, 256], replicated, may hold values from -0.5 to 0.5
- gate_proj: bfloat16 [128, 128], replicated, may hold values from -0.5 to 0.5
- mix_gain: float32 [128], replicated, may hold values from 0.25 to 1.75
- out_proj: bfloat16 [128, 128], replicated, may hold values from -0.5 to 0.5
- bias_proj: bfloat16 [128, 4], replicated, may hold values from -0.5 to 0.5
- token_single: bfloat16 [768, 384], P('row'), may hold values from -18 to 18
- cond_proj: bfloat16 [384, 128], replicated, may hold values from -0.3125 to 0.3125
- atom_act: bfloat16 [32, 4096, 128], P('col', 'row'), may hold values from -6 to 6
- atom_gain: float32 [128], replicated, may hold values from 0.25 to 1.75
- qkv_proj: bfloat16 [128, 384], replicated, may hold values from -0.5 to 0.5
- attn_proj: bfloat16 [128, 128], replicated, may hold values from -0.5 to 0.5
- token_proj: bfloat16 [128, 768], replicated, may hold values from -0.5 to 0.5
- atom_token: int32 [4096], P('row'), may hold values from 0 to 767, as said below
- atom_mask: int32 [4096], P('row'), may hold values from 0 to 1, as said below
- key_start: int32 [128], P('row'), may hold values from 0 to 3968, as said below
Outputs:
- tri_update: bfloat16 [768, 768, 128], P('row', 'col')
- atom_update: bfloat16 [32, 4096, 128], P('col', 'row')
- token_update: bfloat16 [32, 768, 768], P('col', 'row')
Inputs may be any that keep to these rules, and one draw needn't show every extreme that they name: `atom_token`: slots r * 512 to (r + 1) * 512 - 1 hold atoms of tokens r * 96 to (r + 1) * 96 - 1, in nondecreasing order of token. `atom_mask`: in each block of 512 slots the live slots come first; at least 128 of a block are live. Window w holds the query slots 32 * w to 32 * w + 31; key_start[w] lies between 32 * w - 64 and 32 * w - 32, moved into the range.
All inputs are finite; a program needn't handle non-finite values.
Results may differ from a plain program's by a relative error of at most 0.024.
The roundings to bfloat16 on the way count: a program that leaves them out, or rounds other values in their place, can miss the bound.
Values may be sent and summed in bfloat16 or wider, within the bound.
A program may use at most 192 MiB of HBM per device.

v0:
```python
import math

import jax
import jax.numpy as jnp
from jax import lax
from jax.sharding import PartitionSpec as P

HEADS = 4
QWIN = 32
KWIN = 128
HALO = 64


def with_halo(cells, sides, width):
    for axis, dim in sides:
        count = lax.axis_size(axis)
        ends = count - 1
        head = lax.slice_in_dim(cells, 0, width, axis=dim)
        tail = lax.slice_in_dim(cells, cells.shape[dim] - width, cells.shape[dim], axis=dim)
        cells = jnp.concatenate(
            [
                lax.ppermute(tail, axis, [(i, (i + 1) % count) for i in range(ends)]),
                cells,
                lax.ppermute(head, axis, [((i + 1) % count, i) for i in range(ends)]),
            ],
            axis=dim,
        )
    return cells


def layer_norm(values, gain):
    centre = values - jnp.mean(values, axis=-1, keepdims=True)
    spread = jnp.mean(centre * centre, axis=-1, keepdims=True)
    return centre * lax.rsqrt(spread + 1e-05) * gain


def gated_proj(normed, weight, channels):
    joined = jnp.dot(normed, weight, preferred_element_type=jnp.float32)
    return (jax.nn.sigmoid(joined[:, :channels]) * joined[:, channels:]).astype(jnp.bfloat16)


def body(
    pair_act,
    pair_gain,
    left_proj,
    right_proj,
    gate_proj,
    mix_gain,
    out_proj,
    bias_proj,
    token_single,
    cond_proj,
    atom_act,
    atom_gain,
    qkv_proj,
    attn_proj,
    token_proj,
    atom_token,
    atom_mask,
    key_start,
):
    row_count, col_count, channels = pair_act.shape
    pair_norm = layer_norm(pair_act.astype(jnp.float32), pair_gain).astype(jnp.bfloat16)
    flat_norm = pair_norm.reshape(row_count * col_count, channels)
    left_side = gated_proj(flat_norm, left_proj, channels).reshape(row_count, col_count, channels)
    right_side = gated_proj(flat_norm, right_proj, channels).reshape(row_count, col_count, channels)
    gate_vals = jax.nn.sigmoid(jnp.dot(flat_norm, gate_proj, preferred_element_type=jnp.float32))
    right_all = lax.all_gather(right_side, "row", axis=0, tiled=True)
    mixed_sum = jnp.transpose(
        lax.psum_scatter(
            jnp.einsum(
                "jkc,ikc->jic", right_all, left_side, preferred_element_type=jnp.float32
            ).astype(jnp.bfloat16),
            "col",
            scatter_dimension=0,
            tiled=True,
        ).astype(jnp.float32),
        (1, 0, 2),
    )
    mixed_norm = layer_norm(mixed_sum, mix_gain).astype(jnp.bfloat16)
    projected = jnp.dot(
        mixed_norm.reshape(row_count * col_count, channels),
        out_proj,
        preferred_element_type=jnp.float32,
    )
    tri_update = (
        (gate_vals * projected).astype(jnp.bfloat16).reshape(row_count, col_count, channels)
    )
    updated_pair = (pair_act.astype(jnp.float32) + tri_update.astype(jnp.float32)).astype(
        jnp.bfloat16
    )
    local_bias = jnp.dot(
        updated_pair.reshape(row_count * col_count, channels),
        bias_proj,
        preferred_element_type=jnp.float32,
    ).reshape(row_count, col_count, HEADS)
    bias_rows = lax.all_gather(local_bias.astype(jnp.bfloat16), "col", axis=1, tiled=True).astype(
        local_bias.dtype
    )
    total_tokens = bias_rows.shape[1]
    block_index = lax.axis_index("row")
    token_rows = token_single.shape[0]
    sample_count, slot_count, atom_width = atom_act.shape
    head_dim = atom_width // HEADS
    local_token = atom_token - block_index * token_rows
    token_hot = (local_token[:, None] == jnp.arange(token_rows, dtype=jnp.int32)[None, :]).astype(
        jnp.bfloat16
    )
    cond_token = jnp.dot(token_single, cond_proj, preferred_element_type=jnp.float32).astype(
        jnp.bfloat16
    )
    atom_cond = jnp.dot(token_hot, cond_token, preferred_element_type=jnp.float32)
    atom_hidden = (layer_norm(atom_act.astype(jnp.float32), atom_gain) + atom_cond[None]).astype(
        jnp.bfloat16
    )
    flat_hidden = atom_hidden.reshape(sample_count * slot_count, atom_width)
    key_code = jnp.where(atom_mask > 0, atom_token + 1, 0)
    code_ext = with_halo(key_code, (("row", 0),), HALO)
    qkv_all = (
        jnp.dot(flat_hidden, qkv_proj, preferred_element_type=jnp.float32)
        .astype(jnp.bfloat16)
        .reshape(sample_count, slot_count, 3 * atom_width)
    )
    queries = qkv_all[:, :, :atom_width]
    kv_ext = with_halo(qkv_all[:, :, atom_width:], (("row", 1),), HALO)
    win_offsets = key_start - block_index * slot_count + HALO
    win_count = win_offsets.shape[0]
    kv_win = jax.vmap(lambda offset: lax.dynamic_slice_in_dim(kv_ext, offset, KWIN, 1))(win_offsets)
    code_win = jax.vmap(lambda offset: lax.dynamic_slice_in_dim(code_ext, offset, KWIN, 0))(
        win_offsets
    )
    query_bias = jnp.dot(
        token_hot.astype(jnp.float32),
        bias_rows.reshape(token_rows, total_tokens * HEADS),
        precision=lax.Precision.HIGHEST,
    ).reshape(win_count, QWIN, total_tokens, HEADS)
    key_hot = (
        (code_win - 1)[:, :, None] == jnp.arange(total_tokens, dtype=jnp.int32)[None, None, :]
    ).astype(jnp.float32)
    window_bias = jnp.einsum("wqjh,wkj->whqk", query_bias, key_hot, precision=lax.Precision.HIGHEST)
    query_heads = queries.reshape(sample_count, win_count, QWIN, HEADS, head_dim)
    key_heads = kv_win[:, :, :, :atom_width].reshape(win_count, sample_count, KWIN, HEADS, head_dim)
    value_heads = kv_win[:, :, :, atom_width:].reshape(
        win_count, sample_count, KWIN, HEADS, head_dim
    )
    scores = (
        jnp.einsum("swqhd,wskhd->swhqk", query_heads, key_heads, preferred_element_type=jnp.float32)
        / math.sqrt(head_dim)
        + window_bias[None]
    )
    key_live = code_win > 0
    scores = jnp.where(key_live[None, :, None, None, :], scores, -1000000000.0)
    row_peak = jnp.max(scores, axis=-1, keepdims=True)
    raised = jnp.exp(scores - row_peak)
    weights = (raised / jnp.sum(raised, axis=-1, keepdims=True)).astype(jnp.bfloat16)
    attended = (
        jnp.einsum("swhqk,wskhd->swqhd", weights, value_heads, preferred_element_type=jnp.float32)
        .astype(jnp.bfloat16)
        .reshape(sample_count * slot_count, atom_width)
    )
    slot_live = (atom_mask > 0).astype(jnp.float32)
    atom_update = (
        jnp.dot(attended, attn_proj, preferred_element_type=jnp.float32).reshape(
            sample_count, slot_count, atom_width
        )
        * slot_live[None, :, None]
    ).astype(jnp.bfloat16)
    token_terms = (
        jax.nn.relu(
            jnp.dot(
                atom_update.reshape(sample_count * slot_count, atom_width),
                token_proj,
                preferred_element_type=jnp.float32,
            )
        )
        .astype(jnp.bfloat16)
        .reshape(sample_count, slot_count, token_proj.shape[1])
    )
    live_hot = token_hot * slot_live.astype(jnp.bfloat16)[:, None]
    token_sums = jnp.einsum(
        "lr,slc->src", live_hot, token_terms, preferred_element_type=jnp.float32
    )
    counts = jnp.sum(live_hot.astype(jnp.float32), axis=0)
    token_update = (token_sums / jnp.maximum(counts, 1.0)[None, :, None]).astype(jnp.bfloat16)
    return (tri_update, atom_update, token_update)


def solution(mesh):
    placed = (
        P("row", "col", None),
        P(),
        P(),
        P(),
        P(),
        P(),
        P(),
        P(),
        P("row", None),
        P(),
        P("col", "row", None),
        P(),
        P(),
        P(),
        P(),
        P("row"),
        P("row"),
        P("row"),
    )
    return jax.shard_map(
        body,
        mesh=mesh,
        in_specs=placed,
        out_specs=(P("row", "col", None), P("col", "row", None), P("col", "row", None)),
        check_vma=False,
    )
```

profile of v0, /device:TPU:17, one launch (start us, length us, event | category | flops | bytes accessed | tf_op | source)
XLA Modules:
  0.0 297.6 jit_solution(11422104945235248985)
XLA Ops:
  7.2 1.5 convert_reduce_fusion
  8.8 1.8 fusion.25
  11.9 1.1 fusion.29
  14.5 61.2 %all-gather.2.cloned.1.call-done = bf16[768,24,128]{2,1,0:T(8,128)(2,1)} async-done(((bf16[96,24,128]{2,1,0:T(8,128)(2,1)}), bf16[768,24,128]{2,1,0:T(8,128)(2,1)}) %all-gather.2.cloned.1.call-update) | async-done | bytes 4718608 | tf_op jit(solution)/shard_map/all_gather | solution.py:68
  75.7 7.6 %copy.45 = bf16[768,24,128]{0,1,2:T(8,128)(2,1)} copy(bf16[768,24,128]{2,1,0:T(8,128)(2,1)} %all-gather.2.cloned.1.call-done) | data formatting | bytes 9437184 | tf_op jit(solution)/shard_map/all_gather | solution.py:68
  83.3 10.8 %convert_bitcast_fusion = bf16[768,96,128]{0,1,2:T(8,128)(2,1)} fusion(bf16[96,24,128]{0,1,2:T(8,128)(2,1)S(1)} %copy.44, bf16[768,24,128]{0,1,2:T(8,128)(2,1)} %copy.45), kind=kOutput, calls=%fused_computation.5 | convolution fusion | flops 462422016 | bytes 24182784 | tf_op jit(solution)/shard_map/jkc,ikc->jic/dot_general | solution.py:71
  94.1 26.7 %copy.46 = bf16[768,96,128]{2,1,0:T(8,128)(2,1)} copy(bf16[768,96,128]{0,1,2:T(8,128)(2,1)} %convert_bitcast_fusion) | data formatting | bytes 37748736 | tf_op jit(solution)/shard_map/convert_element_type | solution.py:73
  122.8 1.4 collective-permute-start
  124.2 1.3 collective-permute-start.1
  125.6 4.0 %collective-permute-start.2 = (s32[64]{0:T(128)S(1)}, s32[64]{0:T(128)S(1)}, u32[]{:S(2)}, u32[]{:S(2)}) collective-permute-start(s32[64]{0:T(128)S(1)} %get-tuple-element.41), channel_id=1, source_target_pairs={{0,32},{32,64},{64,96},{96,128},{128,160},{160,192},{192,224},{1,3... | collective-permute-start | bytes 776 | tf_op jit(solution)/shard_map/ppermute | solution.py:22
  129.6 1.5 collective-permute-start.3
  132.0 1.5 fusion.6
  134.8 20.0 %while.5 = (s32[]{:T(128)}, s32[640]{0:T(1024)S(1)}, s32[16,1]{0,1:T(1,128)S(1)}, s32[16,128]{1,0:T(8,128)S(1)}) while((s32[]{:T(128)}, s32[640]{0:T(1024)S(1)}, s32[16,1]{0,1:T(1,128)S(1)}, s32[16,128]{1,0:T(8,128)S(1)}) %tuple.45), condition=%wide.while_cond.1.clone, body=%wide.while_body.1.sunk.clone | while | flops 2 | bytes 2121 | solution.py:129
  154.9 20.6 %while.4 = (s32[]{:T(128)}, bf16[1,640,256]{2,1,0:T(8,128)(2,1)S(1)}, s32[16,3]{0,1:T(4,128)S(1)}, bf16[16,1,128,256]{3,2,1,0:T(8,128)(2,1)S(1)}) while((s32[]{:T(128)}, bf16[1,640,256]{2,1,0:T(8,128)(2,1)S(1)}, s32[16,3]{0,1:T(4,128)S(1)}, bf16[16,1,128,256]{3,2,1,0:T(8,128)(2,1)S(1)}) %tuple.42), condition=%wide.while_cond.clone, body=%wide.while_body.sunk.clone | while | flops 2 | bytes 131169 | solution.py:128
  177.3 70.0 %reduce-scatter.2.cloned.1.call-done = bf16[24,96,128]{2,1,0:T(8,128)(2,1)} async-done(((bf16[768,96,128]{2,1,0:T(8,128)(2,1)}), bf16[24,96,128]{2,1,0:T(8,128)(2,1)}) %reduce-scatter.2.cloned.1.call-update) | async-done | bytes 589840 | tf_op jit(solution)/shard_map/reduce_scatter | solution.py:70
  247.3 1.5 bitcast_reduce_fusion
  248.8 1.9 fusion.39
  250.7 1.2 fusion.41
  252.6 1.1 convolution_convert_fusion.2
  253.9 24.8 %all_gather.7 = bf16[96,768,4]{0,2,1:T(4,128)(2,1)S(1)} all-gather(bf16[96,24,4]{0,2,1:T(4,128)(2,1)S(1)} %copy.51), channel_id=1, replica_groups=mesh['row'=8,'col'=32] {'col'}, dimensions={1}, use_global_device_ids=true | all-gather | bytes 608256 | tf_op jit(solution)/shard_map/all_gather | solution.py:97
  279.2 1.0 fusion.52
  280.3 3.9 %fusion.19 = f32[16,4,32,128]{3,2,1,0:T(8,128)S(1)} fusion(f32[16,4,32,128]{3,2,1,0:T(8,128)S(1)} %convolution_multiply_fusion.1, f32[16,32,768,4]{2,1,3,0:T(8,128)S(1)} %fusion.52, s32[16,128]{1,0:T(8,128)S(1)} %broadcast_add_fusion, pred[16,128]{1,0:T(8,128)(4,1)S(1)} %broadcast_compare_fusion), kind=kOutput, calls=%fused_computation.26 | convolution fusion | flops 2418016256 | bytes 8398848 | tf_op jit(solution)/shard_map/wqjh,wkj->whqk/dot_general | solution.py:140
  284.9 3.6 %fusion.23 = bf16[1,16,32,4,32]{2,4,3,1,0:T(8,128)(2,1)S(1)} fusion(bf16[16,128,4,32]{1,3,2,0:T(8,128)(2,1)S(1)} %bitcast.140, f32[16,4,32]{2,1,0:T(4,128)S(1)} %fusion.77, f32[16,4,32,128]{3,2,1,0:T(8,128)S(1)} %fusion.19), kind=kOutput, calls=%fused_computation.31 | convolution fusion | flops 17631360 | bytes 1712128 | tf_op jit(solution)/shard_map/swhqk,wskhd->swqhd/dot_general | solution.py:157
  289.6 1.2 fusion.49
  (198 shorter events, 51.9 us)
Async XLA Ops:
  7.2 282.4 %copy-start = (bf16[128,768]{1,0:T(8,128)(2,1)S(1)}, bf16[128,768]{1,0:T(8,128)(2,1)}, u32[]{:S(2)}) copy-start(bf16[128,768]{1,0:T(8,128)(2,1)} %param.32) | copy-start | bytes 589828
  7.2 3.4 %copy-start.1 = (bf16[96,24,128]{2,1,0:T(8,128)(2,1)S(1)}, bf16[96,24,128]{2,1,0:T(8,128)(2,1)}, u32[]{:S(2)}) copy-start(bf16[96,24,128]{2,1,0:T(8,128)(2,1)} %param.18) | copy-start | bytes 1769476
  7.2 3.4 %copy-start.17 = (f32[128]{0:T(128)S(1)}, f32[128]{0:T(128)}, u32[]{:S(2)}) copy-start(f32[128]{0:T(128)} %param.19) | copy-start | bytes 1540
  7.2 68.5 %all-gather.2.cloned.1.call-start = ((), (), s32[]{:S(2)}) async-start(), calls=%async_computation.1 | async-start | bytes 5308416 | tf_op jit(solution)/shard_map/all_gather | solution.py:68
  8.8 2.7 copy-start.10
  13.0 234.2 %reduce-scatter.2.cloned.1.call-start = ((), (), s32[]{:S(2)}) async-start(), calls=%async_computation.2 | async-start | bytes 19464192 | tf_op jit(solution)/shard_map/reduce_scatter | solution.py:70
  120.8 1.3 copy-start.14
  120.8 1.3 copy-start.19
  120.8 1.3 copy-start.20
  120.9 1.3 copy-start.22
  120.9 1.7 copy-start.9
  120.9 10.9 %copy-start.23 = (s32[16]{0:T(128)S(1)}, s32[16]{0:T(128)}, u32[]{:S(2)}) copy-start(s32[16]{0:T(128)} %param.35) | copy-start | bytes 196
  120.9 11.1 %copy-start.21 = (bf16[128,128]{1,0:T(8,128)(2,1)S(1)}, bf16[128,128]{1,0:T(8,128)(2,1)}, u32[]{:S(2)}) copy-start(bf16[128,128]{1,0:T(8,128)(2,1)} %param.22) | copy-start | bytes 98308
  122.8 32.0 %collective-permute-start = (bf16[1,64,256]{2,1,0:T(8,128)(2,1)S(1)}, bf16[1,64,256]{2,1,0:T(8,128)(2,1)S(1)}, u32[]{:S(2)}, u32[]{:S(2)}) collective-permute-start(bf16[1,64,256]{2,1,0:T(8,128)(2,1)S(1)} %get-tuple-element.39), channel_id=1, source_target_pairs={{0,32},{32,64},{64,96},{96,128},{128,160},{160,192},{192,224},{1,3... | collective-permute-start | bytes 98312 | tf_op jit(solution)/shard_map/ppermute | solution.py:22
  124.2 30.6 %collective-permute-start.1 = (bf16[1,64,256]{2,1,0:T(8,128)(2,1)S(1)}, bf16[1,64,256]{2,1,0:T(8,128)(2,1)S(1)}, u32[]{:S(2)}, u32[]{:S(2)}) collective-permute-start(bf16[1,64,256]{2,1,0:T(8,128)(2,1)S(1)} %get-tuple-element.40), channel_id=1, source_target_pairs={{32,0},{64,32},{96,64},{128,96},{160,128},{192,160},{224,192},{33,... | collective-permute-start | bytes 98312 | tf_op jit(solution)/shard_map/ppermute | solution.py:24
  125.6 8.2 %collective-permute-start.2 = (s32[64]{0:T(128)S(1)}, s32[64]{0:T(128)S(1)}, u32[]{:S(2)}, u32[]{:S(2)}) collective-permute-start(s32[64]{0:T(128)S(1)} %get-tuple-element.41), channel_id=1, source_target_pairs={{0,32},{32,64},{64,96},{96,128},{128,160},{160,192},{192,224},{1,3... | collective-permute-start | bytes 776 | tf_op jit(solution)/shard_map/ppermute | solution.py:22
  129.6 5.1 %collective-permute-start.3 = (s32[64]{0:T(128)S(1)}, s32[64]{0:T(128)S(1)}, u32[]{:S(2)}, u32[]{:S(2)}) collective-permute-start(s32[64]{0:T(128)S(1)} %get-tuple-element.42), channel_id=1, source_target_pairs={{32,0},{64,32},{96,64},{128,96},{160,128},{192,160},{224,192},{33,... | collective-permute-start | bytes 776 | tf_op jit(solution)/shard_map/ppermute | solution.py:24
  133.5 21.3 %copy-start.5 = (bf16[1,512,256]{2,1,0:T(8,128)(2,1)S(1)}, bf16[1,512,256]{2,1,0:T(8,128)(2,1)}, u32[]{:S(2)}) copy-start(bf16[1,512,256]{2,1,0:T(8,128)(2,1)} %slice.76) | copy-start | bytes 786436
  177.3 73.4 %copy-start.18 = (f32[128]{0:T(128)S(1)}, f32[128]{0:T(128)}, u32[]{:S(2)}) copy-start(f32[128]{0:T(128)} %param.23) | copy-start | bytes 1540
  247.3 3.5 %copy-start.2 = (bf16[24,96,128]{2,1,0:T(8,128)(2,1)S(1)}, bf16[24,96,128]{2,1,0:T(8,128)(2,1)}, u32[]{:S(2)}) copy-start(bf16[24,96,128]{2,1,0:T(8,128)(2,1)} %reduce-scatter.2.cloned.1.call-done) | copy-start | bytes 1769476
  248.8 3.1 %copy-start.4 = (f32[2304,128]{1,0:T(8,128)S(1)}, f32[2304,128]{1,0:T(8,128)}, u32[]{:S(2)}) copy-start(f32[2304,128]{1,0:T(8,128)} %fusion.6) | copy-start | bytes 3538948
  248.8 3.1 %copy-start.12 = (bf16[128,128]{1,0:T(8,128)(2,1)S(1)}, bf16[128,128]{1,0:T(8,128)(2,1)}, u32[]{:S(2)}) copy-start(bf16[128,128]{1,0:T(8,128)(2,1)} %param.24) | copy-start | bytes 98308
  252.3 26.9 %copy-start.3 = (bf16[2304,128]{1,0:T(8,128)(2,1)}, bf16[2304,128]{1,0:T(8,128)(2,1)S(1)}, u32[]{:S(2)}) copy-start(bf16[2304,128]{1,0:T(8,128)(2,1)S(1)} %fusion.7) | copy-start | bytes 1769476
  280.3 4.6 %copy-start.6 = (bf16[16,1,128,128]{2,3,0,1:T(8,128)(2,1)S(1)}, bf16[16,1,128,128]{2,3,0,1:T(8,128)(2,1)}, u32[]{:S(2)}) copy-start(bf16[16,1,128,128]{2,3,0,1:T(8,128)(2,1)} %copy.48) | copy-start | bytes 1572868
  (6 other events, 6.1 us)
Sparse Core Ops, SparseCore 0:
  13.2 62.5 all-gather.1
  121.0 126.2 reduce-scatter.1
where the time goes:
time: 302 us; the launch traced here: 298 us
  waiting for transfers between devices  132 us (44%)
  local copies, waits for them, and re-layouts  80.5 us (27%)
  matrix products  25.5 us (8%)
  blocking collectives  24.8 us (8%)
  between operations  14.7 us (5%)
  other arithmetic  11.4 us (4%)
  starting transfers between devices  8.21 us (3%)
    reduce_scatter x1, waiting for transfers between devices, body(): lax.psum_scatter(jnp.einsum('jkc,ikc->jic', right_all, left_side, preferr...  70 us
    all_gather x1, waiting for transfers between devices, body(): right_all = lax.all_gather(right_side, 'row', axis=0, tiled=True)  61.2 us
    gather x96, local copies, waits for them, and re-layouts  40.1 us
    convert_element_type x1, local copies, waits for them, and re-layouts, body(): mixed_sum = jnp.transpose(lax.psum_scatter(jnp.einsum('jkc,ikc->jic', rig...  26.7 us
    all_gather x1, blocking collectives, body(): lax.all_gather(local_bias.astype(jnp.bfloat16), 'col', axis=1, tiled=True)  24.8 us
    dot_general x1, matrix products, body(): jnp.einsum('jkc,ikc->jic', right_all, left_side, preferred_element_type=j...  10.8 us
    all_gather x1, local copies, waits for them, and re-layouts, body(): right_all = lax.all_gather(right_side, 'row', axis=0, tiled=True)  7.61 us
  transfers between devices with their start and end apart: 6, of which 3 were waited for; matrix products, arithmetic and copies ran while one was open for 16% of the time, Pallas kernels for 0%

commit v1 on v0

v1 whole, which is shorter than its diff:
```python
import functools
import math

import jax
import jax.numpy as jnp
from jax import lax
from jax.experimental import pallas as pl
from jax.experimental.pallas import tpu as pltpu
from jax.sharding import PartitionSpec as P

MESH = pl.DeviceIdType.MESH
HEADS = 4
QWIN = 32
KWIN = 128
HALO = 64
LANES = 128
F32 = jnp.float32
BF16 = jnp.bfloat16
NT = (((1,), (1,)), ((), ()))
TN = (((0,), (0,)), ((), ()))


def dot(a, b, dims=None):
    if dims is None:
        return jnp.dot(a, b, preferred_element_type=F32)
    return lax.dot_general(a, b, dims, preferred_element_type=F32)


def normalised(values, axis):
    centre = values - jnp.mean(values, axis=axis, keepdims=True)
    spread = jnp.mean(centre * centre, axis=axis, keepdims=True)
    return centre * lax.rsqrt(spread + 1e-05)


def wait_bytes(ref, sem):
    pltpu.make_async_copy(ref, ref, sem).wait()


def padded(rows):
    return jnp.concatenate([rows, jnp.zeros((LANES - rows.shape[0], rows.shape[1]), rows.dtype)], axis=0)


def kernel(
    n_row,
    n_col,
    rt,
    cw,
    x_ref,
    pgain_ref,
    lproj_ref,
    rproj_ref,
    gproj_ref,
    mgain_ref,
    oproj_ref,
    bproj_ref,
    single_ref,
    cproj_ref,
    atom_ref,
    again_ref,
    qkvproj_ref,
    aproj_ref,
    tproj_ref,
    tok_ref,
    mask_ref,
    start_ref,
    tri_ref,
    aupd_ref,
    tupd_ref,
    xf,
    xn,
    wt,
    side_f,
    side_r,
    side_l,
    recv_r,
    recv_l,
    rtr,
    lt,
    ring,
    mf,
    msend,
    mrecv,
    mrf,
    gate,
    trif,
    biasf,
    bias_out,
    bias_in,
    bm,
    gcol,
    bpt,
    code,
    tokq,
    q_s,
    kv,
    att,
    sem_r,
    sem_l,
    sem_out,
    ring_send,
    ring_recv,
    m_send,
    m_recv,
    b_send,
    b_recv,
    halo_send,
    halo_recv,
):
    r = lax.axis_index("row")
    q = lax.axis_index("col")
    cpd = LANES // n_col
    half = cpd // 2
    sub = rt // cw
    blk = cpd * cw
    hb = half * cw
    right = lax.rem(r + 1, n_row)
    left = lax.rem(r + n_row - 1, n_row)
    slots = atom_ref.shape[0]
    far = n_row // 2

    def to_col(target, src, dst, send, recv):
        return pltpu.make_async_remote_copy(
            src_ref=src, dst_ref=dst, send_sem=send, recv_sem=recv, device_id={"col": target}, device_id_type=MESH
        )

    def to_row(target, src, dst, send, recv):
        return pltpu.make_async_remote_copy(
            src_ref=src, dst_ref=dst, send_sem=send, recv_sem=recv, device_id={"row": target}, device_id_type=MESH
        )

    barrier = pltpu.get_barrier_semaphore()

    def greet(d, _):
        pl.semaphore_signal(barrier, inc=1, device_id={"col": lax.rem(q + d, n_col)}, device_id_type=MESH)
        return 0

    lax.fori_loop(1, n_col, greet, 0)
    pl.semaphore_signal(barrier, inc=1, device_id={"row": right}, device_id_type=MESH)
    pl.semaphore_signal(barrier, inc=1, device_id={"row": left}, device_id_type=MESH)

    pgain = pgain_ref[...]

    def norm_step(t, _):
        rows = pl.ds(pl.multiple_of(t * rt, rt), rt)
        v = x_ref[rows, :].astype(F32)
        xf[rows, :] = v
        xn[rows, :] = normalised(v, -1) * pgain
        return 0

    lax.fori_loop(0, cw, norm_step, 0, unroll=2)

    def column(k):
        return padded(xn[pl.ds(k, rt, stride=cw), :].astype(BF16))

    def gated(xk):
        joined = dot(wt[...], xk, NT)
        return jax.nn.sigmoid(joined[:LANES]) * joined[LANES:]

    def pack(dst):
        def step(t, _):
            rows = pl.ds(pl.multiple_of(t * 384, 384), 384)
            dst[rows, :] = side_f[rows, :].astype(BF16)
            return 0

        lax.fori_loop(0, LANES * cw // 384, step, 0, unroll=2)

    def spread_half(src, dst, sem, h):
        def step(d, _):
            target = lax.rem(q + d, n_col)
            to_col(
                target,
                src.at[pl.ds(pl.multiple_of(target * blk + h * hb, 16), hb)],
                dst.at[h, pl.ds(pl.multiple_of(q * hb, 16), hb)],
                sem_out.at[0],
                sem.at[h],
            ).start()
            return 0

        lax.fori_loop(1, n_col, step, 0)
        pltpu.make_async_copy(
            src.at[pl.ds(pl.multiple_of(q * blk + h * hb, 16), hb)],
            dst.at[h, pl.ds(pl.multiple_of(q * hb, 16), hb)],
            sem.at[h],
        ).start()

    wt[...] = rproj_ref[...].astype(F32).T.astype(BF16)

    def right_step(k, _):
        side_f[pl.ds(k, LANES, stride=cw), :] = gated(column(k))
        return 0

    lax.fori_loop(0, cw, right_step, 0, unroll=2)
    pack(side_r)
    pl.semaphore_wait(barrier, n_col + 1)
    spread_half(side_r, recv_r, sem_r, 0)
    spread_half(side_r, recv_r, sem_r, 1)

    wt[...] = lproj_ref[...].astype(F32).T.astype(BF16)
    gproj = gproj_ref[...]

    def left_step(k, _):
        xk = column(k)
        side_f[pl.ds(k, LANES, stride=cw), :] = gated(xk)
        gate[k] = jax.nn.sigmoid(dot(xk, gproj))[:rt]
        return 0

    lax.fori_loop(0, cw, left_step, 0, unroll=2)
    pack(side_l)
    spread_half(side_l, recv_l, sem_l, 0)
    spread_half(side_l, recv_l, sem_l, 1)

    def channel_rows(src, h, p, c):
        pair = src[h, pl.ds(pl.multiple_of(p * 2 * hb, 16), 2 * hb), :].astype(F32)
        return jnp.concatenate([pair[c * cw : (c + 1) * cw], pair[hb + c * cw : hb + (c + 1) * cw]], axis=0)

    def ring_chunk(s, c):
        return ring.at[s, c]

    def forward(direction, s, c, src):
        target = right if direction == 0 else left
        dst = s + 1 if (direction == 0 or s + 1 == far) else far + s + 1
        return to_row(target, src, ring.at[dst, c], ring_send.at[direction, s, c], ring_recv.at[direction, s + 1, c])

    for h in range(2):
        wait_bytes(recv_r.at[h], sem_r.at[h])
        for cc in range(half):
            c = h * half + cc

            def gather_step(p, _, cc=cc, h=h):
                rtr[pl.ds(pl.multiple_of(p * 2 * cw, 16), 2 * cw), :] = channel_rows(recv_r, h, p, cc)
                return 0

            lax.fori_loop(0, n_col // 2, gather_step, 0, unroll=4)
            for b in range(n_col * cw // LANES):
                ring[0, c, :, b * LANES : (b + 1) * LANES] = rtr[b * LANES : (b + 1) * LANES, :].T[:rt].astype(BF16)
            forward(0, 0, c, ring.at[0, c]).start()
            forward(1, 0, c, ring.at[0, c]).start()

    lane = lax.broadcasted_iota(jnp.int32, (LANES, LANES), 1)
    first = (r * rt).astype(F32)
    code_rows = jnp.where(mask_ref[...] > 0, tok_ref[...] + 1, 0).astype(F32)
    tok_rows = tok_ref[...].astype(F32) - first
    cond = padded(dot(single_ref[...], cproj_ref[...]).astype(BF16))
    lane_f = lane.astype(F32)
    again = again_ref[...]
    for g in range(slots // LANES):
        rows = slice(g * LANES, (g + 1) * LANES)
        code[HALO + g * LANES : HALO + (g + 1) * LANES, :] = jnp.broadcast_to(code_rows[g : g + 1], (LANES, LANES)).T
        tcol = jnp.broadcast_to(tok_rows[g : g + 1], (LANES, LANES)).T
        hot = (tcol == lane_f).astype(F32).astype(BF16)
        hidden = (normalised(atom_ref[rows, :].astype(F32), -1) * again + dot(hot, cond)).astype(BF16)
        joined = dot(hidden, qkvproj_ref[...]).astype(BF16)
        q_s[rows, :] = joined[:, :LANES]
        kv[HALO + g * LANES : HALO + (g + 1) * LANES, :] = joined[:, LANES:]
    group = lax.broadcasted_iota(jnp.int32, tok_rows.shape, 1) // QWIN
    per_row = LANES // QWIN
    for g in range(per_row):
        own = jnp.where(group == g, tok_rows, 0.0)
        tiled = own + pltpu.roll(own, QWIN, 1) + pltpu.roll(own, 2 * QWIN, 1) + pltpu.roll(own, 3 * QWIN, 1)
        tokq[pl.ds(g, slots // LANES, stride=per_row), :] = tiled + (group * LANES).astype(F32)
    halos = []
    for n, buf in enumerate((kv, code)):
        halos.append(
            to_row(right, buf.at[pl.ds(slots, HALO)], buf.at[pl.ds(0, HALO)], halo_send.at[n, 0], halo_recv.at[n, 0])
        )
        halos.append(
            to_row(left, buf.at[pl.ds(HALO, HALO)], buf.at[pl.ds(HALO + slots, HALO)], halo_send.at[n, 1], halo_recv.at[n, 1])
        )
    for copy in halos:
        copy.start()

    for h in range(2):
        wait_bytes(recv_l.at[h], sem_l.at[h])
        for cc in range(half):

            def left_gather(p, _, cc=cc, h=h):
                lt[h * half + cc, pl.ds(pl.multiple_of(p * 2 * cw, 16), 2 * cw), :] = channel_rows(recv_l, h, p, cc).astype(BF16)
                return 0

            lax.fori_loop(0, n_col // 2, left_gather, 0, unroll=4)

    gcol[...] = jnp.broadcast_to(mgain_ref[...], (LANES, LANES)).T
    bpt[...] = jnp.concatenate([bproj_ref[...].astype(F32), jnp.zeros((LANES, LANES - HEADS), F32)], axis=1).T[:8].astype(BF16)

    def multiply(slot, c, d):
        m = dot(ring[slot, c], lt[c])
        for s in range(sub):
            mf[d, (s * cpd + c) * cw : (s * cpd + c + 1) * cw, :] = m[s * cw : (s + 1) * cw]

    def send_block(slot, d, source):
        msend[slot] = mf[d].astype(BF16)
        for s in range(sub):
            target = source * sub + s
            src = msend.at[slot, pl.ds(s * blk, blk)]
            dst = mrecv.at[pl.ds(pl.multiple_of(q * blk, 16), blk)]

            @pl.when(target == q)
            def _():
                pltpu.make_async_copy(src, dst, m_recv).start()

            @pl.when(target != q)
            def _():
                to_col(target, src, dst, m_send, m_recv).start()

    def finish(with_bias):
        wait_bytes(mrecv, m_recv)

        def widen(t, _):
            rows = pl.ds(pl.multiple_of(t * 384, 384), 384)
            mrf[rows, :] = mrecv[rows, :].astype(F32)
            return 0

        lax.fori_loop(0, LANES * cw // 384, widen, 0, unroll=2)
        oproj = oproj_ref[...]

        def step(j, _):
            v = mrf[pl.ds(j, LANES, stride=cw), :]
            n = (normalised(v, 0) * gcol[...]).astype(BF16)
            projected = dot(n, oproj, TN)[:rt]
            tri = (gate[j] * projected).astype(BF16).astype(F32)
            trif[pl.ds(j, rt, stride=cw), :] = tri
            if with_bias:
                updated = (xf[pl.ds(j, rt, stride=cw), :] + tri).astype(BF16)
                biasf[pl.ds(j, HEADS, stride=cw), :] = dot(bpt[...], padded(updated), NT)[:HEADS]
            return 0

        lax.fori_loop(0, cw, step, 0, unroll=2)

        def narrow(t, _):
            rows = pl.ds(pl.multiple_of(t * 384, 384), 384)
            tri_ref[rows, :] = trif[rows, :].astype(BF16)
            return 0

        lax.fori_loop(0, rt * cw // 384, narrow, 0, unroll=2)

    owner = q // sub
    near = lax.rem(owner - r + 1 + n_row, n_row)
    is_near = near < 3

    def step_in(direction, s, c):
        slot = s if (direction == 0 or s == far) else far + s
        wait_bytes(ring.at[slot, c], ring_recv.at[direction, s, c])
        if s + 1 < far or (s + 1 == far and (c < half) == (direction == 0)):
            forward(direction, s, c, ring.at[slot, c]).start()
        multiply(slot, c, direction)

    for c in range(cpd):
        multiply(0, c, 0)
    send_block(0, 0, r)

    for s in range(1, far):
        for c in range(cpd):
            step_in(0, s, c)
            step_in(1, s, c)
        send_block(s, 0, lax.rem(r + n_row - s, n_row))
        send_block(far + s, 1, lax.rem(r + s, n_row))
        if s == 1:

            @pl.when(is_near)
            def _():
                finish(True)
                bias_out[...] = biasf[...].astype(BF16)
                dst = bias_in.at[pl.ds(pl.multiple_of((near * sub + lax.rem(q, sub)) * HEADS * cw, 16), HEADS * cw)]

                def share(d, _):
                    to_col(lax.rem(q + d, n_col), bias_out, dst, b_send, b_recv).start()
                    return 0

                lax.fori_loop(1, n_col, share, 0)
                pltpu.make_async_copy(bias_out, dst, b_recv).start()

        if s == 2:
            attend(
                n_row, r, rt, cw, sub, slots, bias_in, b_recv, bm, code, tokq, q_s, kv, att, halos, start_ref,
                aproj_ref, tproj_ref, code_rows, aupd_ref, tupd_ref,
            )
    for c in range(half):
        step_in(0, far, c)
        step_in(1, far, c + half)
    merge = half * cw
    for s in range(sub):
        mf[0, s * blk + merge : (s + 1) * blk, :] = mf[1, s * blk + merge : (s + 1) * blk, :]
    send_block(far, 0, lax.rem(r + far, n_row))

    @pl.when(jnp.logical_not(is_near))
    def _():
        finish(False)

    for _ in range(2):
        wait_bytes(side_r.at[pl.ds(0, (n_col - 1) * blk)], sem_out.at[0])
    wait_bytes(mrecv.at[pl.ds(0, (n_col - 1) * blk)], m_send)

    @pl.when(is_near)
    def _():
        wait_bytes(mrecv.at[pl.ds(0, (n_col - 1) * HEADS * cw)], b_send)

    for direction in range(2):
        for s in range(far):
            for c in range(cpd):
                if s + 1 < far or (c < half) == (direction == 0):
                    wait_bytes(ring.at[0, c], ring_send.at[direction, s, c])
    for copy in halos:
        copy.wait_send()


def attend(
    n_row, r, rt, cw, sub, slots, bias_in, b_recv, bm, code, tokq, q_s, kv, att, halos, start_ref, aproj_ref, tproj_ref,
    code_rows, aupd_ref, tupd_ref,
):
    hq = HEADS * QWIN
    span = QWIN + KWIN
    windows = slots // QWIN
    hb = HEADS * cw
    for copy in halos:
        copy.wait_recv()
    wait_bytes(bias_in, b_recv)
    count = 3 * sub
    for p in range(count // 2):
        pair = bias_in[p * 2 * hb : (p + 1) * 2 * hb, :].astype(F32)
        heads = [
            jnp.concatenate([pair[h * cw : (h + 1) * cw], pair[hb + h * cw : hb + (h + 1) * cw]], axis=0)
            for h in range(HEADS)
        ]
        bm[p * 2 * cw : (p + 1) * 2 * cw, :] = jnp.concatenate(heads, axis=1).astype(BF16)
    bm[count * cw :, :] = jnp.zeros((bm.shape[0] - count * cw, bm.shape[1]), BF16)
    wide = bm.shape[0]
    row_head = lax.broadcasted_iota(jnp.int32, (hq, LANES), 0) // QWIN
    col_head = lax.broadcasted_iota(jnp.int32, (hq, LANES), 1) // (LANES // HEADS)
    own_head = row_head == col_head
    pick = lax.broadcasted_iota(jnp.int32, (HEADS * LANES, LANES), 0).astype(F32)
    place = lax.broadcasted_iota(jnp.int32, (span, LANES), 0)
    tokens = lax.broadcasted_iota(jnp.int32, (span, LANES), 1).astype(F32) + ((r - 1) * rt + 1).astype(F32)
    scale = 1.0 / math.sqrt(LANES // HEADS)

    def window(w, _):
        at = pl.multiple_of(w * QWIN, QWIN)
        first = (1 - (r + n_row - 1) // n_row) * (1 - (w + windows - 1) // windows)
        last = ((r + 1) // n_row) * ((w + 1) // windows)
        base = pl.multiple_of((w + first - last) * QWIN, QWIN)
        kw = kv[pl.ds(base, span), :LANES]
        vw = kv[pl.ds(base, span), LANES:]
        qw = q_s[pl.ds(at, QWIN), :]
        qm = jnp.where(own_head, jnp.concatenate([qw] * HEADS, axis=0).astype(F32), 0.0).astype(BF16)
        hot_q = (pick == tokq[pl.ds(w, 1), :]).astype(F32).astype(BF16)
        bias_q = dot(bm[...], hot_q).astype(BF16)
        cw_code = code[pl.ds(base, span), :]
        hot_k = jnp.concatenate(
            [(cw_code == tokens + float(t * LANES)).astype(F32) for t in range(wide // LANES)], axis=1
        ).astype(BF16)
        scores = dot(kw, qm, NT) * scale + dot(hot_k, bias_q)
        begin = start_ref[w] - r * slots + HALO - base
        valid = (cw_code > 0.0) & (place >= begin) & (place < begin + KWIN)
        scores = jnp.where(valid, scores, -1000000000.0)
        raised = jnp.exp(scores - jnp.max(scores, axis=0, keepdims=True))
        weights = (raised / jnp.sum(raised, axis=0, keepdims=True)).astype(BF16)
        mixed = jnp.where(own_head, dot(weights, vw, TN), 0.0)
        total = mixed[:QWIN]
        for h in range(1, HEADS):
            total = total + mixed[h * QWIN : (h + 1) * QWIN]
        att[pl.ds(at, QWIN), :] = total.astype(BF16)
        return 0

    lax.fori_loop(0, windows, window, 0, unroll=2)

    live = code[HALO : HALO + slots, :] > 0.0
    updated = jnp.where(live, dot(att[...], aproj_ref[...]), 0.0).astype(BF16)
    aupd_ref[...] = updated
    terms = jnp.maximum(dot(updated, tproj_ref[...]), 0.0).astype(BF16)
    own = (lax.broadcasted_iota(jnp.int32, (rt, LANES), 0) + r * rt + 1).astype(F32)
    hot = jnp.concatenate(
        [(own == code_rows[g : g + 1]).astype(F32) for g in range(slots // LANES)], axis=1
    )
    counts = jnp.maximum(jnp.sum(hot, axis=1, keepdims=True), 1.0)
    tupd_ref[...] = (dot(hot.astype(BF16), terms) / counts).astype(BF16)


def body(n_row, n_col, *args):
    (
        pair_act, pair_gain, left_proj, right_proj, gate_proj, mix_gain, out_proj, bias_proj, token_single, cond_proj,
        atom_act, atom_gain, qkv_proj, attn_proj, token_proj, atom_token, atom_mask, key_start,
    ) = args
    rt, cw, channels = pair_act.shape
    cpd = channels // n_col
    sub = rt // cw
    slots = atom_act.shape[1]
    far = n_row // 2
    depth = n_col * cw
    blk = cpd * cw
    vmem = pl.BlockSpec(memory_space=pltpu.VMEM)
    smem = pl.BlockSpec(memory_space=pltpu.SMEM)
    dma = pltpu.SemaphoreType.DMA
    rows = rt * cw
    scratch = [
        pltpu.VMEM((rows, LANES), F32),
        pltpu.VMEM((rows, LANES), F32),
        pltpu.VMEM((2 * LANES, LANES), BF16),
        pltpu.VMEM((LANES * cw, LANES), F32),
        pltpu.VMEM((LANES * cw, LANES), BF16),
        pltpu.VMEM((LANES * cw, LANES), BF16),
        pltpu.VMEM((2, n_col * blk // 2, LANES), BF16),
        pltpu.VMEM((2, n_col * blk // 2, LANES), BF16),
        pltpu.VMEM((depth, LANES), F32),
        pltpu.VMEM((cpd, depth, LANES), BF16),
        pltpu.VMEM((2 * far, cpd, rt, depth), BF16),
        pltpu.VMEM((2, sub * blk, LANES), F32),
        pltpu.VMEM((2 * far, sub * blk, LANES), BF16),
        pltpu.VMEM((LANES * cw, LANES), BF16),
        pltpu.VMEM((LANES * cw, LANES), F32),
        pltpu.VMEM((cw, rt, LANES), F32),
        pltpu.VMEM((rows, LANES), F32),
        pltpu.VMEM((HEADS * cw, LANES), F32),
        pltpu.VMEM((HEADS * cw, LANES), BF16),
        pltpu.VMEM((3 * sub * HEADS * cw, LANES), BF16),
        pltpu.VMEM((-(-3 * rt // LANES) * LANES, HEADS * LANES), BF16),
        pltpu.VMEM((LANES, LANES), F32),
        pltpu.VMEM((8, LANES), BF16),
        pltpu.VMEM((slots + 2 * HALO, LANES), F32),
        pltpu.VMEM((slots // QWIN, LANES), F32),
        pltpu.VMEM((slots, LANES), BF16),
        pltpu.VMEM((slots + 2 * HALO, 2 * LANES), BF16),
        pltpu.VMEM((slots, LANES), BF16),
        dma((2,)),
        dma((2,)),
        dma((1,)),
        dma((2, far, cpd)),
        dma((2, far + 1, cpd)),
        dma,
        dma,
        dma,
        dma,
        dma((2, 2)),
        dma((2, 2)),
    ]
    tri, aupd, tupd = pl.pallas_call(
        functools.partial(kernel, n_row, n_col, rt, cw),
        out_shape=[
            jax.ShapeDtypeStruct((rows, channels), BF16),
            jax.ShapeDtypeStruct((slots, channels), BF16),
            jax.ShapeDtypeStruct((rt, token_proj.shape[1]), BF16),
        ],
        in_specs=[vmem] * 17 + [smem],
        out_specs=[vmem] * 3,
        scratch_shapes=scratch,
        compiler_params=pltpu.CompilerParams(collective_id=0, has_side_effects=True, vmem_limit_bytes=56 * 1024 * 1024),
        name="triangle_attention",
    )(
        pair_act.reshape(rows, channels), pair_gain.reshape(1, -1), left_proj, right_proj, gate_proj, mix_gain.reshape(1, -1),
        out_proj, bias_proj, token_single, cond_proj, atom_act.reshape(slots, channels), atom_gain.reshape(1, -1), qkv_proj,
        attn_proj, token_proj, atom_token.reshape(-1, LANES), atom_mask.reshape(-1, LANES), key_start,
    )
    return tri.reshape(pair_act.shape), aupd.reshape(atom_act.shape), tupd[None]


def solution(mesh):
    none = P()
    row = P("row")
    atoms = P("col", "row", None)
    pair = P("row", "col", None)
    placed = (pair,) + (none,) * 7 + (P("row", None), none, atoms) + (none,) * 4 + (row,) * 3
    return jax.shard_map(
        functools.partial(body, mesh.shape["row"], mesh.shape["col"]),
        mesh=mesh,
        in_specs=placed,
        out_specs=(pair, atoms, atoms),
        check_vma=False,
    )
```

time: 302 us -> 101 us (0.33); the launches traced: 298 us -> 100 us
  waiting for transfers between devices: 132 us -> 0 us
  Pallas kernels: 0 us -> 94.5 us
  local copies, waits for them, and re-layouts: 80.5 us -> 5 us
  matrix products: 25.5 us -> 0 us
  blocking collectives: 24.8 us -> 0 us
  between operations: 14.7 us -> 0.66 us
  other arithmetic: 11.4 us -> 0 us
  starting transfers between devices: 8.21 us -> 0 us
    pallas_call x0 -> x1, Pallas kernels: none -> 94.5 us  [body(): pl.pallas_call(functools.partial(kernel, n_row, n_col, rt, cw), out_shape...]
    reduce_scatter x1 -> x0, waiting for transfers between devices: 70 us -> none  [body(): lax.psum_scatter(jnp.einsum('jkc,ikc->jic', right_all, left_side, preferr...]
    all_gather x1 -> x0, waiting for transfers between devices: 61.2 us -> none  [body(): right_all = lax.all_gather(right_side, 'row', axis=0, tiled=True)]
    gather x96 -> x0, local copies, waits for them, and re-layouts: 40.1 us -> none
    convert_element_type x3 -> x0, local copies, waits for them, and re-layouts: 27.2 us -> none  [the longest x1 26.7 us: body(): mixed_sum = jnp.transpose(lax.psum_scatter(jnp.einsum('jkc,ikc->jic', rig...]
    dot_general x14 -> x0, matrix products: 25.5 us -> none  [the longest x1 10.8 us: body(): jnp.einsum('jkc,ikc->jic', right_all, left_side, preferred_element_type=j...]
    all_gather x1 -> x0, blocking collectives: 24.8 us -> none  [body(): lax.all_gather(local_bias.astype(jnp.bfloat16), 'col', axis=1, tiled=True)]
    ppermute x4 -> x0, starting transfers between devices: 8.13 us -> none  [the longest x2 5.37 us: with_halo(): lax.ppermute(tail, axis, [(i, (i + 1) % count) for i in range(ends)])]
  transfers between devices with their start and end apart: 6 -> 0, of which waited for: 3 -> 0; matrix products, arithmetic and copies ran while one was open for 16% -> 0% of each run, Pallas kernels for 0% -> 0%
where the time goes in v1:
time: 101 us; the launch traced here: 100 us
  Pallas kernels  94.5 us (94%)
  local copies, waits for them, and re-layouts  5 us (5%)
    pallas_call x1, Pallas kernels, body(): pl.pallas_call(functools.partial(kernel, n_row, n_col, rt, cw), out_shape...  94.5 us
    unnamed x10, local copies, waits for them, and re-layouts  5 us

profile of v1, /device:TPU:17, one launch (start us, length us, event | category | flops | bytes accessed | tf_op | source)
XLA Modules:
  0.0 100.1 jit_solution(4772251800740516701)
XLA Ops:
  0.6 0.0 copy-start.2
  0.6 0.7 copy-done.2
  1.3 0.7 copy.21.bproj_ref
  2.0 94.5 %triangle_attention.1 = (bf16[2304,128]{1,0:T(8,128)(2,1)}, bf16[512,128]{1,0:T(8,128)(2,1)}, bf16[96,768]{1,0:T(8,128)(2,1)}) custom-call(bf16[2304,128]{1,0:T(8,128)(2,1)} %bitcast.10, f32[1,128]{1,0:T(1,128)} %bitcast.17, bf16[128,256]{1,0:T(8,128)(2,1)} %lproj_ref.1, bf16[128,256]{1,0:T(8,128)(2,1)} %rproj_ref.1, bf16[128,128]{1,0:T(8,128)(2,1)} %gproj_ref.1, ...), custom_call_target="tpu_custom_call" | custom-call | tf_op jit(solution)/shard_map/triangle_attention/pallas_call | solution.py:534
  96.5 0.0 copy-start.1
  96.5 2.0 %copy.25 = bf16[96,24,128]{2,1,0:T(8,128)(2,1)} copy(bf16[96,24,128]{2,1,0:T(8,128)(2,1)} %bitcast.11) | data formatting | bytes 1179648
  98.5 0.0 copy-done.1
  98.5 0.0 copy-start
  98.5 0.7 copy.26
  99.2 0.3 copy-done
  99.5 0.7 copy.27
Async XLA Ops:
  0.6 0.7 copy-start.2
  96.5 2.0 %copy-start.1 = (bf16[512,128]{1,0:T(8,128)(2,1)S(1)}, bf16[512,128]{1,0:T(8,128)(2,1)}, u32[]{:S(2)}) copy-start(bf16[512,128]{1,0:T(8,128)(2,1)} %get-tuple-element.7) | copy-start | bytes 393220
  98.5 1.0 copy-start

commit v2 on v1

--- a/solution.py
+++ b/solution.py
@@ -213,14 +213,6 @@
         pair = src[h, pl.ds(pl.multiple_of(p * 2 * hb, 16), 2 * hb), :].astype(F32)
         return jnp.concatenate([pair[c * cw : (c + 1) * cw], pair[hb + c * cw : hb + (c + 1) * cw]], axis=0)
 
-    def ring_chunk(s, c):
-        return ring.at[s, c]
-
-    def forward(direction, s, c, src):
-        target = right if direction == 0 else left
-        dst = s + 1 if (direction == 0 or s + 1 == far) else far + s + 1
-        return to_row(target, src, ring.at[dst, c], ring_send.at[direction, s, c], ring_recv.at[direction, s + 1, c])
-
     for h in range(2):
         wait_bytes(recv_r.at[h], sem_r.at[h])
         for cc in range(half):
@@ -233,8 +225,8 @@
             lax.fori_loop(0, n_col // 2, gather_step, 0, unroll=4)
             for b in range(n_col * cw // LANES):
                 ring[0, c, :, b * LANES : (b + 1) * LANES] = rtr[b * LANES : (b + 1) * LANES, :].T[:rt].astype(BF16)
-            forward(0, 0, c, ring.at[0, c]).start()
-            forward(1, 0, c, ring.at[0, c]).start()
+            to_row(right, ring.at[0, c], ring.at[1, c], ring_send.at[0, 0, c], ring_recv.at[0, 1, c]).start()
+            to_row(left, ring.at[0, c], ring.at[far + 1, c], ring_send.at[1, 0, c], ring_recv.at[1, 1, c]).start()
 
     lane = lax.broadcasted_iota(jnp.int32, (LANES, LANES), 1)
     first = (r * rt).astype(F32)
@@ -269,30 +261,32 @@
     for copy in halos:
         copy.start()
 
-    for h in range(2):
-        wait_bytes(recv_l.at[h], sem_l.at[h])
-        for cc in range(half):
-
-            def left_gather(p, _, cc=cc, h=h):
-                lt[h * half + cc, pl.ds(pl.multiple_of(p * 2 * cw, 16), 2 * cw), :] = channel_rows(recv_l, h, p, cc).astype(BF16)
+    def gather_left():
+        for h in range(2):
+            wait_bytes(recv_l.at[h], sem_l.at[h])
+
+            def left_gather(p, _, h=h):
+                for cc in range(half):
+                    lt[h * half + cc, pl.ds(pl.multiple_of(p * 2 * cw, 16), 2 * cw), :] = channel_rows(recv_l, h, p, cc).astype(BF16)
                 return 0
 
-            lax.fori_loop(0, n_col // 2, left_gather, 0, unroll=4)
+            lax.fori_loop(0, n_col // 2, left_gather, 0, unroll=2)
 
     gcol[...] = jnp.broadcast_to(mgain_ref[...], (LANES, LANES)).T
-    bpt[...] = jnp.concatenate([bproj_ref[...].astype(F32), jnp.zeros((LANES, LANES - HEADS), F32)], axis=1).T[:8].astype(BF16)
+    bpt[...] = jnp.concatenate([bproj_ref[...].astype(F32), jnp.zeros((8 - HEADS, LANES), F32)], axis=0).astype(BF16)
 
     def multiply(slot, c, d):
         m = dot(ring[slot, c], lt[c])
         for s in range(sub):
-            mf[d, (s * cpd + c) * cw : (s * cpd + c + 1) * cw, :] = m[s * cw : (s + 1) * cw]
-
-    def send_block(slot, d, source):
+            mf[d, pl.ds(pl.multiple_of((s * cpd + c) * cw, 8), cw), :] = m[s * cw : (s + 1) * cw]
+
+    def send_block(slot, d, source, first, size):
         msend[slot] = mf[d].astype(BF16)
-        for s in range(sub):
+
+        def step(s, _):
             target = source * sub + s
-            src = msend.at[slot, pl.ds(s * blk, blk)]
-            dst = mrecv.at[pl.ds(pl.multiple_of(q * blk, 16), blk)]
+            src = msend.at[slot, pl.ds(pl.multiple_of(s * blk + first, 16), size)]
+            dst = mrecv.at[pl.ds(pl.multiple_of(q * blk + first, 16), size)]
 
             @pl.when(target == q)
             def _():
@@ -302,7 +296,49 @@
             def _():
                 to_col(target, src, dst, m_send, m_recv).start()
 
-    def finish(with_bias):
+            return 0
+
+        lax.fori_loop(0, sub, step, 0)
+
+    owner = q // sub
+    near = lax.rem(owner - r + 1 + n_row, n_row)
+    is_near = near < 3
+    final = (far - 1) * cpd
+    events = final + half
+    early = 3
+    finish_at = cpd + 1
+    attend_at = final - 4
+    portion = slots // QWIN // 4
+
+    def place(e):
+        s = e // cpd + 1
+        c = lax.rem(e, cpd)
+        last = e // final
+        c0 = c + last * c
+        return s, c0, c0 + last, s + far * (1 - last), last
+
+    def pass_on(e):
+        s, c0, c1, slot1, last = place(e)
+        wait_bytes(ring.at[s, c0], ring_recv.at[0, s, c0])
+        before = (s + 1) // far
+
+        @pl.when((last == 0) & (before * lax.rem(c0, 2) == 0))
+        def _():
+            to_row(right, ring.at[s, c0], ring.at[s + 1, c0], ring_send.at[0, s, c0], ring_recv.at[0, s + 1, c0]).start()
+
+        wait_bytes(ring.at[slot1, c1], ring_recv.at[1, s, c1])
+
+        @pl.when((last == 0) & (before * lax.rem(c0 + 1, 2) == 0))
+        def _():
+            to_row(
+                left,
+                ring.at[slot1, c1],
+                ring.at[s + 1 + far * (1 - before), c1],
+                ring_send.at[1, s, c1],
+                ring_recv.at[1, s + 1, c1],
+            ).start()
+
+    def finish():
         wait_bytes(mrecv, m_recv)
 
         def widen(t, _):
@@ -317,14 +353,28 @@
             v = mrf[pl.ds(j, LANES, stride=cw), :]
             n = (normalised(v, 0) * gcol[...]).astype(BF16)
             projected = dot(n, oproj, TN)[:rt]
-            tri = (gate[j] * projected).astype(BF16).astype(F32)
-            trif[pl.ds(j, rt, stride=cw), :] = tri
-            if with_bias:
-                updated = (xf[pl.ds(j, rt, stride=cw), :] + tri).astype(BF16)
+            trif[pl.ds(j, rt, stride=cw), :] = (gate[j] * projected).astype(BF16).astype(F32)
+            return 0
+
+        lax.fori_loop(0, cw, step, 0, unroll=4)
+
+        @pl.when(is_near)
+        def _():
+            def bias_step(j, _):
+                updated = (xf[pl.ds(j, rt, stride=cw), :] + trif[pl.ds(j, rt, stride=cw), :]).astype(BF16)
                 biasf[pl.ds(j, HEADS, stride=cw), :] = dot(bpt[...], padded(updated), NT)[:HEADS]
-            return 0
-
-        lax.fori_loop(0, cw, step, 0, unroll=2)
+                return 0
+
+            lax.fori_loop(0, cw, bias_step, 0, unroll=2)
+            bias_out[...] = biasf[...].astype(BF16)
+            dst = bias_in.at[pl.ds(pl.multiple_of((near * sub + lax.rem(q, sub)) * HEADS * cw, 16), HEADS * cw)]
+
+            def share(d, _):
+                to_col(lax.rem(q + d, n_col), bias_out, dst, b_send, b_recv).start()
+                return 0
+
+            lax.fori_loop(1, n_col, share, 0)
+            pltpu.make_async_copy(bias_out, dst, b_recv).start()
 
         def narrow(t, _):
             rows = pl.ds(pl.multiple_of(t * 384, 384), 384)
@@ -333,58 +383,64 @@
 
         lax.fori_loop(0, rt * cw // 384, narrow, 0, unroll=2)
 
-    owner = q // sub
-    near = lax.rem(owner - r + 1 + n_row, n_row)
-    is_near = near < 3
-
-    def step_in(direction, s, c):
-        slot = s if (direction == 0 or s == far) else far + s
-        wait_bytes(ring.at[slot, c], ring_recv.at[direction, s, c])
-        if s + 1 < far or (s + 1 == far and (c < half) == (direction == 0)):
-            forward(direction, s, c, ring.at[slot, c]).start()
-        multiply(slot, c, direction)
-
-    for c in range(cpd):
+    def early_step(e, _):
+        pass_on(e)
+        return 0
+
+    lax.fori_loop(0, early, early_step, 0)
+    gather_left()
+
+    def own_step(c, _):
         multiply(0, c, 0)
-    send_block(0, 0, r)
-
-    for s in range(1, far):
-        for c in range(cpd):
-            step_in(0, s, c)
-            step_in(1, s, c)
-        send_block(s, 0, lax.rem(r + n_row - s, n_row))
-        send_block(far + s, 1, lax.rem(r + s, n_row))
-        if s == 1:
-
-            @pl.when(is_near)
+        return 0
+
+    lax.fori_loop(0, cpd, own_step, 0)
+    send_block(0, 0, r, 0, blk)
+
+    prepare, window, conclude = attention(
+        n_row, r, rt, cw, sub, slots, bias_in, b_recv, bm, code, tokq, q_s, kv, att, halos, start_ref, aproj_ref, tproj_ref,
+        code_rows, aupd_ref, tupd_ref,
+    )
+
+    def event(e, _):
+        @pl.when((e >= early) & (e < events))
+        def _():
+            pass_on(e)
+
+        @pl.when(e < events)
+        def _():
+            s, c0, c1, slot1, last = place(e)
+            multiply(s, c0, 0)
+            multiply(slot1, c1, 1 - last)
+
+            @pl.when((last == 0) & (c0 == cpd - 1))
             def _():
-                finish(True)
-                bias_out[...] = biasf[...].astype(BF16)
-                dst = bias_in.at[pl.ds(pl.multiple_of((near * sub + lax.rem(q, sub)) * HEADS * cw, 16), HEADS * cw)]
-
-                def share(d, _):
-                    to_col(lax.rem(q + d, n_col), bias_out, dst, b_send, b_recv).start()
-                    return 0
-
-                lax.fori_loop(1, n_col, share, 0)
-                pltpu.make_async_copy(bias_out, dst, b_recv).start()
-
-        if s == 2:
-            attend(
-                n_row, r, rt, cw, sub, slots, bias_in, b_recv, bm, code, tokq, q_s, kv, att, halos, start_ref,
-                aproj_ref, tproj_ref, code_rows, aupd_ref, tupd_ref,
-            )
-    for c in range(half):
-        step_in(0, far, c)
-        step_in(1, far, c + half)
-    merge = half * cw
-    for s in range(sub):
-        mf[0, s * blk + merge : (s + 1) * blk, :] = mf[1, s * blk + merge : (s + 1) * blk, :]
-    send_block(far, 0, lax.rem(r + far, n_row))
-
-    @pl.when(jnp.logical_not(is_near))
-    def _():
-        finish(False)
+                send_block(s, 0, lax.rem(r + n_row - s, n_row), 0, blk)
+                send_block(slot1, 1, lax.rem(r + s, n_row), 0, blk)
+
+            @pl.when(last == 1)
+            def _():
+                send_block(far + far * (e - final), 0, lax.rem(r + far, n_row), (e - final) * hb, hb)
+
+        @pl.when(e == attend_at)
+        def _():
+            prepare()
+
+        @pl.when((e >= attend_at) & (e < attend_at + 4))
+        def _():
+            lax.fori_loop((e - attend_at) * portion, (e - attend_at + 1) * portion, window, 0)
+
+        @pl.when(e == events)
+        def _():
+            conclude()
+
+        @pl.when(e == jnp.where(is_near, finish_at, events))
+        def _():
+            finish()
+
+        return 0
+
+    lax.fori_loop(0, events + 1, event, 0)
 
     for _ in range(2):
         wait_bytes(side_r.at[pl.ds(0, (n_col - 1) * blk)], sem_out.at[0])
@@ -394,16 +450,21 @@
     def _():
         wait_bytes(mrecv.at[pl.ds(0, (n_col - 1) * HEADS * cw)], b_send)
 
-    for direction in range(2):
-        for s in range(far):
-            for c in range(cpd):
-                if s + 1 < far or (c < half) == (direction == 0):
-                    wait_bytes(ring.at[0, c], ring_send.at[direction, s, c])
+    def ring_left(n, _):
+        s = n // cpd
+        c = lax.rem(n, cpd)
+        wait_bytes(ring.at[0, c], ring_send.at[0, s, c])
+        wait_bytes(ring.at[0, c], ring_send.at[1, s, c])
+        return 0
+
+    lax.fori_loop(0, final, ring_left, 0)
+    for c in range(cpd):
+        wait_bytes(ring.at[0, c], ring_send.at[c % 2, far - 1, c])
     for copy in halos:
         copy.wait_send()
 
 
-def attend(
+def attention(
     n_row, r, rt, cw, sub, slots, bias_in, b_recv, bm, code, tokq, q_s, kv, att, halos, start_ref, aproj_ref, tproj_ref,
     code_rows, aupd_ref, tupd_ref,
 ):
@@ -411,18 +472,20 @@
     span = QWIN + KWIN
     windows = slots // QWIN
     hb = HEADS * cw
-    for copy in halos:
-        copy.wait_recv()
-    wait_bytes(bias_in, b_recv)
-    count = 3 * sub
-    for p in range(count // 2):
-        pair = bias_in[p * 2 * hb : (p + 1) * 2 * hb, :].astype(F32)
-        heads = [
-            jnp.concatenate([pair[h * cw : (h + 1) * cw], pair[hb + h * cw : hb + (h + 1) * cw]], axis=0)
-            for h in range(HEADS)
-        ]
-        bm[p * 2 * cw : (p + 1) * 2 * cw, :] = jnp.concatenate(heads, axis=1).astype(BF16)
-    bm[count * cw :, :] = jnp.zeros((bm.shape[0] - count * cw, bm.shape[1]), BF16)
+    def prepare():
+        for copy in halos:
+            copy.wait_recv()
+        wait_bytes(bias_in, b_recv)
+        count = 3 * sub
+        for p in range(count // 2):
+            pair = bias_in[p * 2 * hb : (p + 1) * 2 * hb, :].astype(F32)
+            heads = [
+                jnp.concatenate([pair[h * cw : (h + 1) * cw], pair[hb + h * cw : hb + (h + 1) * cw]], axis=0)
+                for h in range(HEADS)
+            ]
+            bm[p * 2 * cw : (p + 1) * 2 * cw, :] = jnp.concatenate(heads, axis=1).astype(BF16)
+        bm[count * cw :, :] = jnp.zeros((bm.shape[0] - count * cw, bm.shape[1]), BF16)
+
     wide = bm.shape[0]
     row_head = lax.broadcasted_iota(jnp.int32, (hq, LANES), 0) // QWIN
     col_head = lax.broadcasted_iota(jnp.int32, (hq, LANES), 1) // (LANES // HEADS)
@@ -460,18 +523,31 @@
         att[pl.ds(at, QWIN), :] = total.astype(BF16)
         return 0
 
-    lax.fori_loop(0, windows, window, 0, unroll=2)
-
-    live = code[HALO : HALO + slots, :] > 0.0
-    updated = jnp.where(live, dot(att[...], aproj_ref[...]), 0.0).astype(BF16)
-    aupd_ref[...] = updated
-    terms = jnp.maximum(dot(updated, tproj_ref[...]), 0.0).astype(BF16)
-    own = (lax.broadcasted_iota(jnp.int32, (rt, LANES), 0) + r * rt + 1).astype(F32)
-    hot = jnp.concatenate(
-        [(own == code_rows[g : g + 1]).astype(F32) for g in range(slots // LANES)], axis=1
-    )
-    counts = jnp.maximum(jnp.sum(hot, axis=1, keepdims=True), 1.0)
-    tupd_ref[...] = (dot(hot.astype(BF16), terms) / counts).astype(BF16)
+    def conclude():
+
+        live = code[HALO : HALO + slots, :] > 0.0
+        updated = jnp.where(live, dot(att[...], aproj_ref[...]), 0.0).astype(BF16)
+        aupd_ref[...] = updated
+        terms = jnp.maximum(dot(updated, tproj_ref[...]), 0.0).astype(BF16)
+        own = (lax.broadcasted_iota(jnp.int32, (rt, LANES), 0) + r * rt + 1).astype(F32)
+        hot = jnp.concatenate(
+            [(own == code_rows[g : g + 1]).astype(F32) for g in range(slots // LANES)], axis=1
+        )
+        counts = jnp.maximum(jnp.sum(hot, axis=1, keepdims=True), 1.0)
+        tupd_ref[...] = (dot(hot.astype(BF16), terms) / counts).astype(BF16)
+
+    return prepare, window, conclude
+
+
+def hand_over(a_ref, b_ref, c_ref, a_out, b_out, c_out, sems):
+    copies = [
+        pltpu.make_async_copy(src, dst, sems.at[n])
+        for n, (src, dst) in enumerate(((a_ref, a_out), (b_ref, b_out), (c_ref, c_out)))
+    ]
+    for copy in copies:
+        copy.start()
+    for copy in copies:
+        copy.wait()
 
 
 def body(n_row, n_col, *args):
@@ -503,7 +579,7 @@
         pltpu.VMEM((cpd, depth, LANES), BF16),
         pltpu.VMEM((2 * far, cpd, rt, depth), BF16),
         pltpu.VMEM((2, sub * blk, LANES), F32),
-        pltpu.VMEM((2 * far, sub * blk, LANES), BF16),
+        pltpu.VMEM((2 * far + 1, sub * blk, LANES), BF16),
         pltpu.VMEM((LANES * cw, LANES), BF16),
         pltpu.VMEM((LANES * cw, LANES), F32),
         pltpu.VMEM((cw, rt, LANES), F32),
@@ -531,7 +607,7 @@
         dma((2, 2)),
         dma((2, 2)),
     ]
-    tri, aupd, tupd = pl.pallas_call(
+    made = pl.pallas_call(
         functools.partial(kernel, n_row, n_col, rt, cw),
         out_shape=[
             jax.ShapeDtypeStruct((rows, channels), BF16),
@@ -545,9 +621,17 @@
         name="triangle_attention",
     )(
         pair_act.reshape(rows, channels), pair_gain.reshape(1, -1), left_proj, right_proj, gate_proj, mix_gain.reshape(1, -1),
-        out_proj, bias_proj, token_single, cond_proj, atom_act.reshape(slots, channels), atom_gain.reshape(1, -1), qkv_proj,
+        out_proj, bias_proj.T, token_single, cond_proj, atom_act.reshape(slots, channels), atom_gain.reshape(1, -1), qkv_proj,
         attn_proj, token_proj, atom_token.reshape(-1, LANES), atom_mask.reshape(-1, LANES), key_start,
     )
+    tri, aupd, tupd = pl.pallas_call(
+        hand_over,
+        out_shape=[jax.ShapeDtypeStruct(a.shape, a.dtype) for a in made],
+        in_specs=[pl.BlockSpec(memory_space=pl.ANY)] * 3,
+        out_specs=[pl.BlockSpec(memory_space=pl.ANY)] * 3,
+        scratch_shapes=[dma((3,))],
+        name="hand_over",
+    )(*made)
     return tri.reshape(pair_act.shape), aupd.reshape(atom_act.shape), tupd[None]
 
 

time: 101 us -> 113 us (1.12); the launches traced: 100 us -> 113 us
  Pallas kernels: 94.5 us -> 113 us
  local copies, waits for them, and re-layouts: 5 us -> 0 us
    pallas_call x0 -> x1, Pallas kernels: none -> 27.4 us  [body(): pl.pallas_call(hand_over, out_shape=[jax.ShapeDtypeStruct(a.shape, a.dtyp...]
    pallas_call x1, Pallas kernels: 94.5 us -> 85.3 us  [body(): pl.pallas_call(functools.partial(kernel, n_row, n_col, rt, cw), out_shape...]
    unnamed x10 -> x0, local copies, waits for them, and re-layouts: 5 us -> none
where the time goes in v2:
time: 113 us
  Pallas kernels  113 us (100%)
    pallas_call x1, Pallas kernels, body(): pl.pallas_call(functools.partial(kernel, n_row, n_col, rt, cw), out_shape...  85.3 us
    pallas_call x1, Pallas kernels, body(): pl.pallas_call(hand_over, out_shape=[jax.ShapeDtypeStruct(a.shape, a.dtyp...  27.4 us

profile of v2, /device:TPU:17, one launch (start us, length us, event | category | flops | bytes accessed | tf_op | source)
XLA Modules:
  0.0 113.4 jit_solution(9667758738478144300)
XLA Ops:
  0.6 85.3 %triangle_attention.1 = (bf16[2304,128]{1,0:T(8,128)(2,1)}, bf16[512,128]{1,0:T(8,128)(2,1)}, bf16[96,768]{1,0:T(8,128)(2,1)}) custom-call(bf16[2304,128]{1,0:T(8,128)(2,1)} %bitcast.11, f32[1,128]{1,0:T(1,128)} %bitcast.16, bf16[128,256]{1,0:T(8,128)(2,1)} %lproj_ref.1, bf16[128,256]{1,0:T(8,128)(2,1)} %rproj_ref.1, bf16[128,128]{1,0:T(8,128)(2,1)} %gproj_ref.1, ...), custom_call_target="tpu_custom_call" | custom-call | tf_op jit(solution)/shard_map/triangle_attention/pallas_call | solution.py:610
  85.9 27.4 %hand_over.1 = (bf16[2304,128]{1,0:T(8,128)(2,1)}, bf16[512,128]{1,0:T(8,128)(2,1)}, bf16[96,768]{1,0:T(8,128)(2,1)}) custom-call(bf16[2304,128]{1,0:T(8,128)(2,1)} %get-tuple-element.9.a_ref, bf16[512,128]{1,0:T(8,128)(2,1)} %get-tuple-element.10.b_ref, bf16[96,768]{1,0:T(8,128)(2,1)} %get-tuple-element.11.c_ref), custom_call_target="tpu_custom_call" | custom-call | tf_op jit(solution)/shard_map/hand_over/pallas_call | solution.py:627

commit v3 on v2

--- a/solution.py
+++ b/solution.py
@@ -90,7 +90,10 @@
     gcol,
     bpt,
     code,
-    tokq,
+    hot_q,
+    hot_k,
+    scores,
+    bias_q,
     q_s,
     kv,
     att,
@@ -240,16 +243,11 @@
         code[HALO + g * LANES : HALO + (g + 1) * LANES, :] = jnp.broadcast_to(code_rows[g : g + 1], (LANES, LANES)).T
         tcol = jnp.broadcast_to(tok_rows[g : g + 1], (LANES, LANES)).T
         hot = (tcol == lane_f).astype(F32).astype(BF16)
+        hot_q[rows, :] = hot
         hidden = (normalised(atom_ref[rows, :].astype(F32), -1) * again + dot(hot, cond)).astype(BF16)
         joined = dot(hidden, qkvproj_ref[...]).astype(BF16)
         q_s[rows, :] = joined[:, :LANES]
         kv[HALO + g * LANES : HALO + (g + 1) * LANES, :] = joined[:, LANES:]
-    group = lax.broadcasted_iota(jnp.int32, tok_rows.shape, 1) // QWIN
-    per_row = LANES // QWIN
-    for g in range(per_row):
-        own = jnp.where(group == g, tok_rows, 0.0)
-        tiled = own + pltpu.roll(own, QWIN, 1) + pltpu.roll(own, 2 * QWIN, 1) + pltpu.roll(own, 3 * QWIN, 1)
-        tokq[pl.ds(g, slots // LANES, stride=per_row), :] = tiled + (group * LANES).astype(F32)
     halos = []
     for n, buf in enumerate((kv, code)):
         halos.append(
@@ -307,8 +305,8 @@
     events = final + half
     early = 3
     finish_at = cpd + 1
-    attend_at = final - 4
-    portion = slots // QWIN // 4
+    attend_at = final - 3
+    portion = slots // QWIN // 8
 
     def place(e):
         s = e // cpd + 1
@@ -383,8 +381,25 @@
 
         lax.fori_loop(0, rt * cw // 384, narrow, 0, unroll=2)
 
+    ahead, prepare, window, conclude = attention(
+        n_row, r, rt, cw, sub, slots, bias_in, b_recv, bm, bias_q, code, hot_q, hot_k, scores, q_s, kv, att, halos, start_ref,
+        aproj_ref, tproj_ref, code_rows, aupd_ref, tupd_ref,
+    )
+
+    pairs = slots // QWIN // 2
+
     def early_step(e, _):
         pass_on(e)
+
+        @pl.when(e == 1)
+        def _():
+            for copy in halos:
+                copy.wait_recv()
+
+        @pl.when(e > 0)
+        def _():
+            lax.fori_loop((e - 1) * (pairs // 2), e * (pairs // 2), ahead, 0)
+
         return 0
 
     lax.fori_loop(0, early, early_step, 0)
@@ -396,11 +411,6 @@
 
     lax.fori_loop(0, cpd, own_step, 0)
     send_block(0, 0, r, 0, blk)
-
-    prepare, window, conclude = attention(
-        n_row, r, rt, cw, sub, slots, bias_in, b_recv, bm, code, tokq, q_s, kv, att, halos, start_ref, aproj_ref, tproj_ref,
-        code_rows, aupd_ref, tupd_ref,
-    )
 
     def event(e, _):
         @pl.when((e >= early) & (e < events))
@@ -465,88 +475,101 @@
 
 
 def attention(
-    n_row, r, rt, cw, sub, slots, bias_in, b_recv, bm, code, tokq, q_s, kv, att, halos, start_ref, aproj_ref, tproj_ref,
-    code_rows, aupd_ref, tupd_ref,
+    n_row, r, rt, cw, sub, slots, bias_in, b_recv, bm, bias_q, code, hot_q, hot_k, scores, q_s, kv, att, halos, start_ref,
+    aproj_ref, tproj_ref, code_rows, aupd_ref, tupd_ref,
 ):
     hq = HEADS * QWIN
     span = QWIN + KWIN
     windows = slots // QWIN
     hb = HEADS * cw
-    def prepare():
-        for copy in halos:
-            copy.wait_recv()
-        wait_bytes(bias_in, b_recv)
-        count = 3 * sub
-        for p in range(count // 2):
-            pair = bias_in[p * 2 * hb : (p + 1) * 2 * hb, :].astype(F32)
-            heads = [
-                jnp.concatenate([pair[h * cw : (h + 1) * cw], pair[hb + h * cw : hb + (h + 1) * cw]], axis=0)
-                for h in range(HEADS)
-            ]
-            bm[p * 2 * cw : (p + 1) * 2 * cw, :] = jnp.concatenate(heads, axis=1).astype(BF16)
-        bm[count * cw :, :] = jnp.zeros((bm.shape[0] - count * cw, bm.shape[1]), BF16)
-
-    wide = bm.shape[0]
+    count = 3 * sub
+    wide = bm.shape[0] // HEADS
     row_head = lax.broadcasted_iota(jnp.int32, (hq, LANES), 0) // QWIN
     col_head = lax.broadcasted_iota(jnp.int32, (hq, LANES), 1) // (LANES // HEADS)
     own_head = row_head == col_head
-    pick = lax.broadcasted_iota(jnp.int32, (HEADS * LANES, LANES), 0).astype(F32)
     place = lax.broadcasted_iota(jnp.int32, (span, LANES), 0)
     tokens = lax.broadcasted_iota(jnp.int32, (span, LANES), 1).astype(F32) + ((r - 1) * rt + 1).astype(F32)
     scale = 1.0 / math.sqrt(LANES // HEADS)
 
-    def window(w, _):
-        at = pl.multiple_of(w * QWIN, QWIN)
+    def key_base(w):
         first = (1 - (r + n_row - 1) // n_row) * (1 - (w + windows - 1) // windows)
         last = ((r + 1) // n_row) * ((w + 1) // windows)
-        base = pl.multiple_of((w + first - last) * QWIN, QWIN)
+        return pl.multiple_of((w + first - last) * QWIN, QWIN)
+
+    def ahead(w):
+        at = pl.multiple_of(w * QWIN, QWIN)
+        base = key_base(w)
         kw = kv[pl.ds(base, span), :LANES]
-        vw = kv[pl.ds(base, span), LANES:]
         qw = q_s[pl.ds(at, QWIN), :]
         qm = jnp.where(own_head, jnp.concatenate([qw] * HEADS, axis=0).astype(F32), 0.0).astype(BF16)
-        hot_q = (pick == tokq[pl.ds(w, 1), :]).astype(F32).astype(BF16)
-        bias_q = dot(bm[...], hot_q).astype(BF16)
-        cw_code = code[pl.ds(base, span), :]
-        hot_k = jnp.concatenate(
-            [(cw_code == tokens + float(t * LANES)).astype(F32) for t in range(wide // LANES)], axis=1
-        ).astype(BF16)
-        scores = dot(kw, qm, NT) * scale + dot(hot_k, bias_q)
+        key_code = code[pl.ds(base, span), :]
+        for t in range(wide // LANES):
+            hot_k[w, :, t * LANES : (t + 1) * LANES] = (key_code == tokens + float(t * LANES)).astype(F32).astype(BF16)
         begin = start_ref[w] - r * slots + HALO - base
-        valid = (cw_code > 0.0) & (place >= begin) & (place < begin + KWIN)
-        scores = jnp.where(valid, scores, -1000000000.0)
-        raised = jnp.exp(scores - jnp.max(scores, axis=0, keepdims=True))
+        valid = (key_code > 0.0) & (place >= begin) & (place < begin + KWIN)
+        scores[w] = jnp.where(valid, dot(kw, qm, NT) * scale, -1000000000.0)
+
+    def prepare():
+        wait_bytes(bias_in, b_recv)
+        for p in range(count // 2):
+            pair = bias_in[p * 2 * hb : (p + 1) * 2 * hb, :].astype(F32)
+            for h in range(HEADS):
+                rows = jnp.concatenate([pair[h * cw : (h + 1) * cw], pair[hb + h * cw : hb + (h + 1) * cw]], axis=0)
+                bm[h * wide + p * 2 * cw : h * wide + (p + 1) * 2 * cw, :] = rows.astype(BF16)
+        for h in range(HEADS):
+            bm[h * wide + count * cw : (h + 1) * wide, :] = jnp.zeros((wide - count * cw, LANES), BF16)
+
+        def spread(g, _):
+            rows = pl.ds(pl.multiple_of(g * LANES, LANES), LANES)
+            for h in range(HEADS):
+                bias_q[rows, h * wide : (h + 1) * wide] = dot(hot_q[rows, :], bm[h * wide : (h + 1) * wide, :], NT).astype(BF16)
+            return 0
+
+        lax.fori_loop(0, slots // LANES, spread, 0)
+
+    def window(w):
+        at = pl.multiple_of(w * QWIN, QWIN)
+        bias_w = jnp.concatenate([bias_q[pl.ds(at, QWIN), h * wide : (h + 1) * wide] for h in range(HEADS)], axis=0)
+        total = scores[w] + dot(hot_k[w], bias_w, NT)
+        raised = jnp.exp(total - jnp.max(total, axis=0, keepdims=True))
         weights = (raised / jnp.sum(raised, axis=0, keepdims=True)).astype(BF16)
-        mixed = jnp.where(own_head, dot(weights, vw, TN), 0.0)
-        total = mixed[:QWIN]
+        mixed = jnp.where(own_head, dot(weights, kv[pl.ds(key_base(w), span), LANES:], TN), 0.0)
+        out = mixed[:QWIN]
         for h in range(1, HEADS):
-            total = total + mixed[h * QWIN : (h + 1) * QWIN]
-        att[pl.ds(at, QWIN), :] = total.astype(BF16)
-        return 0
+            out = out + mixed[h * QWIN : (h + 1) * QWIN]
+        att[pl.ds(at, QWIN), :] = out.astype(BF16)
 
     def conclude():
-
         live = code[HALO : HALO + slots, :] > 0.0
         updated = jnp.where(live, dot(att[...], aproj_ref[...]), 0.0).astype(BF16)
         aupd_ref[...] = updated
         terms = jnp.maximum(dot(updated, tproj_ref[...]), 0.0).astype(BF16)
         own = (lax.broadcasted_iota(jnp.int32, (rt, LANES), 0) + r * rt + 1).astype(F32)
-        hot = jnp.concatenate(
-            [(own == code_rows[g : g + 1]).astype(F32) for g in range(slots // LANES)], axis=1
-        )
+        hot = jnp.concatenate([(own == code_rows[g : g + 1]).astype(F32) for g in range(slots // LANES)], axis=1)
         counts = jnp.maximum(jnp.sum(hot, axis=1, keepdims=True), 1.0)
         tupd_ref[...] = (dot(hot.astype(BF16), terms) / counts).astype(BF16)
 
-    return prepare, window, conclude
-
-
-def hand_over(a_ref, b_ref, c_ref, a_out, b_out, c_out, sems):
-    copies = [
-        pltpu.make_async_copy(src, dst, sems.at[n])
-        for n, (src, dst) in enumerate(((a_ref, a_out), (b_ref, b_out), (c_ref, c_out)))
-    ]
-    for copy in copies:
+    def in_pairs(work):
+        def step(p, _):
+            work(2 * p)
+            work(2 * p + 1)
+            return 0
+
+        return step
+
+    return in_pairs(ahead), prepare, in_pairs(window), conclude
+
+
+def hand_over(a_ref, b_ref, c_ref, a_out, b_out, c_out, ins, outs, a_mid, b_mid, c_mid):
+    steps = ((a_ref, a_mid, a_out), (b_ref, b_mid, b_out), (c_ref, c_mid, c_out))
+    first = [pltpu.make_async_copy(src, mid, ins.at[n]) for n, (src, mid, _) in enumerate(steps)]
+    then = [pltpu.make_async_copy(mid, dst, outs.at[n]) for n, (_, mid, dst) in enumerate(steps)]
+    for copy in first:
         copy.start()
-    for copy in copies:
+    for came, copy in zip(first, then):
+        came.wait()
+        copy.start()
+    for copy in then:
         copy.wait()
 
 
@@ -566,6 +589,7 @@
     smem = pl.BlockSpec(memory_space=pltpu.SMEM)
     dma = pltpu.SemaphoreType.DMA
     rows = rt * cw
+    wide = -(-3 * rt // LANES) * LANES
     scratch = [
         pltpu.VMEM((rows, LANES), F32),
         pltpu.VMEM((rows, LANES), F32),
@@ -587,11 +611,14 @@
         pltpu.VMEM((HEADS * cw, LANES), F32),
         pltpu.VMEM((HEADS * cw, LANES), BF16),
         pltpu.VMEM((3 * sub * HEADS * cw, LANES), BF16),
-        pltpu.VMEM((-(-3 * rt // LANES) * LANES, HEADS * LANES), BF16),
+        pltpu.VMEM((HEADS * wide, LANES), BF16),
         pltpu.VMEM((LANES, LANES), F32),
         pltpu.VMEM((8, LANES), BF16),
         pltpu.VMEM((slots + 2 * HALO, LANES), F32),
-        pltpu.VMEM((slots // QWIN, LANES), F32),
+        pltpu.VMEM((slots, LANES), BF16),
+        pltpu.VMEM((slots // QWIN, QWIN + KWIN, wide), BF16),
+        pltpu.VMEM((slots // QWIN, QWIN + KWIN, LANES), F32),
+        pltpu.VMEM((slots, HEADS * wide), BF16),
         pltpu.VMEM((slots, LANES), BF16),
         pltpu.VMEM((slots + 2 * HALO, 2 * LANES), BF16),
         pltpu.VMEM((slots, LANES), BF16),
@@ -629,7 +656,7 @@
         out_shape=[jax.ShapeDtypeStruct(a.shape, a.dtype) for a in made],
         in_specs=[pl.BlockSpec(memory_space=pl.ANY)] * 3,
         out_specs=[pl.BlockSpec(memory_space=pl.ANY)] * 3,
-        scratch_shapes=[dma((3,))],
+        scratch_shapes=[dma((3,)), dma((3,))] + [pltpu.VMEM(a.shape, a.dtype) for a in made],
         name="hand_over",
     )(*made)
     return tri.reshape(pair_act.shape), aupd.reshape(atom_act.shape), tupd[None]

time: 113 us -> 88.4 us (0.78); the launches traced: 113 us -> 87.1 us
  Pallas kernels: 113 us -> 86.4 us
    pallas_call x1, Pallas kernels: 27.4 us -> 2.01 us  [body(): pl.pallas_call(hand_over, out_shape=[jax.ShapeDtypeStruct(a.shape, a.dtyp...]
where the time goes in v3:
time: 88.4 us; the launch traced here: 87.1 us
  Pallas kernels  86.4 us (98%)
    pallas_call x1, Pallas kernels, body(): pl.pallas_call(functools.partial(kernel, n_row, n_col, rt, cw), out_shape...  84.4 us
    pallas_call x1, Pallas kernels, body(): pl.pallas_call(hand_over, out_shape=[jax.ShapeDtypeStruct(a.shape, a.dtyp...  2.01 us

profile of v3, /device:TPU:17, one launch (start us, length us, event | category | flops | bytes accessed | tf_op | source)
XLA Modules:
  0.0 87.1 jit_solution(8228410974027410349)
XLA Ops:
  0.6 84.4 %triangle_attention.1 = (bf16[2304,128]{1,0:T(8,128)(2,1)}, bf16[512,128]{1,0:T(8,128)(2,1)}, bf16[96,768]{1,0:T(8,128)(2,1)}) custom-call(bf16[2304,128]{1,0:T(8,128)(2,1)} %bitcast.11, f32[1,128]{1,0:T(1,128)} %bitcast.16, bf16[128,256]{1,0:T(8,128)(2,1)} %lproj_ref.1, bf16[128,256]{1,0:T(8,128)(2,1)} %rproj_ref.1, bf16[128,128]{1,0:T(8,128)(2,1)} %gproj_ref.1, ...), custom_call_target="tpu_custom_call" | custom-call | tf_op jit(solution)/shard_map/triangle_attention/pallas_call | solution.py:637
  85.1 2.0 %hand_over.1 = (bf16[2304,128]{1,0:T(8,128)(2,1)}, bf16[512,128]{1,0:T(8,128)(2,1)}, bf16[96,768]{1,0:T(8,128)(2,1)}) custom-call(bf16[2304,128]{1,0:T(8,128)(2,1)} %get-tuple-element.9.a_ref, bf16[512,128]{1,0:T(8,128)(2,1)} %get-tuple-element.10.b_ref, bf16[96,768]{1,0:T(8,128)(2,1)} %get-tuple-element.11.c_ref), custom_call_target="tpu_custom_call" | custom-call | tf_op jit(solution)/shard_map/hand_over/pallas_call | solution.py:654

commit v4 on v3

--- a/solution.py
+++ b/solution.py
@@ -18,6 +18,10 @@
 BF16 = jnp.bfloat16
 NT = (((1,), (1,)), ((), ()))
 TN = (((0,), (0,)), ((), ()))
+FIRST = (0, 1, 3)
+SECOND = (2, 4)
+THIRD = (5, 6, 7, 8, 9, 10, 11, 12, 13, 14, 15, 16, 17)
+LOAD_ORDER = FIRST + SECOND + THIRD
 
 
 def dot(a, b, dims=None):
@@ -45,24 +49,11 @@
     n_col,
     rt,
     cw,
-    x_ref,
-    pgain_ref,
-    lproj_ref,
-    rproj_ref,
-    gproj_ref,
-    mgain_ref,
-    oproj_ref,
-    bproj_ref,
-    single_ref,
-    cproj_ref,
-    atom_ref,
-    again_ref,
-    qkvproj_ref,
-    aproj_ref,
-    tproj_ref,
-    tok_ref,
-    mask_ref,
-    start_ref,
+    ins,
+    outs,
+    held,
+    in_sems,
+    out_sems,
     tri_ref,
     aupd_ref,
     tupd_ref,
@@ -109,6 +100,13 @@
     halo_send,
     halo_recv,
 ):
+    (
+        x_ref, pgain_ref, lproj_ref, rproj_ref, gproj_ref, mgain_ref, oproj_ref, bproj_ref, single_ref, cproj_ref, atom_ref,
+        again_ref, qkvproj_ref, aproj_ref, tproj_ref, tok_ref, mask_ref, start_ref,
+    ) = held
+    loads = [pltpu.make_async_copy(src, dst, in_sems.at[n]) for n, (src, dst) in enumerate(zip(ins, held))]
+    for n in LOAD_ORDER:
+        loads[n].start()
     r = lax.axis_index("row")
     q = lax.axis_index("col")
     cpd = LANES // n_col
@@ -141,6 +139,9 @@
     pl.semaphore_signal(barrier, inc=1, device_id={"row": right}, device_id_type=MESH)
     pl.semaphore_signal(barrier, inc=1, device_id={"row": left}, device_id_type=MESH)
 
+    for n in FIRST:
+        loads[n].wait()
+
     pgain = pgain_ref[...]
 
     def norm_step(t, _):
@@ -198,6 +199,8 @@
     spread_half(side_r, recv_r, sem_r, 0)
     spread_half(side_r, recv_r, sem_r, 1)
 
+    for n in SECOND:
+        loads[n].wait()
     wt[...] = lproj_ref[...].astype(F32).T.astype(BF16)
     gproj = gproj_ref[...]
 
@@ -230,6 +233,9 @@
                 ring[0, c, :, b * LANES : (b + 1) * LANES] = rtr[b * LANES : (b + 1) * LANES, :].T[:rt].astype(BF16)
             to_row(right, ring.at[0, c], ring.at[1, c], ring_send.at[0, 0, c], ring_recv.at[0, 1, c]).start()
             to_row(left, ring.at[0, c], ring.at[far + 1, c], ring_send.at[1, 0, c], ring_recv.at[1, 1, c]).start()
+
+    for n in THIRD:
+        loads[n].wait()
 
     lane = lax.broadcasted_iota(jnp.int32, (LANES, LANES), 1)
     first = (r * rt).astype(F32)
@@ -278,13 +284,13 @@
         for s in range(sub):
             mf[d, pl.ds(pl.multiple_of((s * cpd + c) * cw, 8), cw), :] = m[s * cw : (s + 1) * cw]
 
-    def send_block(slot, d, source, first, size):
-        msend[slot] = mf[d].astype(BF16)
-
+    def send_half(slot, d, source, h):
         def step(s, _):
             target = source * sub + s
-            src = msend.at[slot, pl.ds(pl.multiple_of(s * blk + first, 16), size)]
-            dst = mrecv.at[pl.ds(pl.multiple_of(q * blk + first, 16), size)]
+            rows = pl.ds(pl.multiple_of(s * blk + h * hb, 16), hb)
+            msend[slot, rows, :] = mf[d, rows, :].astype(BF16)
+            src = msend.at[slot, rows]
+            dst = mrecv.at[pl.ds(pl.multiple_of(q * blk + h * hb, 16), hb)]
 
             @pl.when(target == q)
             def _():
@@ -304,9 +310,9 @@
     final = (far - 1) * cpd
     events = final + half
     early = 3
-    finish_at = cpd + 1
-    attend_at = final - 3
-    portion = slots // QWIN // 8
+    finish_at = cpd + 2
+    attend_at = final - 1
+    pairs = slots // QWIN // 2
 
     def place(e):
         s = e // cpd + 1
@@ -354,7 +360,7 @@
             trif[pl.ds(j, rt, stride=cw), :] = (gate[j] * projected).astype(BF16).astype(F32)
             return 0
 
-        lax.fori_loop(0, cw, step, 0, unroll=4)
+        lax.fori_loop(0, cw, step, 0, unroll=8)
 
         @pl.when(is_near)
         def _():
@@ -363,7 +369,7 @@
                 biasf[pl.ds(j, HEADS, stride=cw), :] = dot(bpt[...], padded(updated), NT)[:HEADS]
                 return 0
 
-            lax.fori_loop(0, cw, bias_step, 0, unroll=2)
+            lax.fori_loop(0, cw, bias_step, 0, unroll=8)
             bias_out[...] = biasf[...].astype(BF16)
             dst = bias_in.at[pl.ds(pl.multiple_of((near * sub + lax.rem(q, sub)) * HEADS * cw, 16), HEADS * cw)]
 
@@ -386,8 +392,6 @@
         aproj_ref, tproj_ref, code_rows, aupd_ref, tupd_ref,
     )
 
-    pairs = slots // QWIN // 2
-
     def early_step(e, _):
         pass_on(e)
 
@@ -410,7 +414,8 @@
         return 0
 
     lax.fori_loop(0, cpd, own_step, 0)
-    send_block(0, 0, r, 0, blk)
+    send_half(0, 0, r, 0)
+    send_half(0, 0, r, 1)
 
     def event(e, _):
         @pl.when((e >= early) & (e < events))
@@ -423,26 +428,29 @@
             multiply(s, c0, 0)
             multiply(slot1, c1, 1 - last)
 
-            @pl.when((last == 0) & (c0 == cpd - 1))
+            @pl.when((last == 1) | (lax.rem(c0 + 1, half) == 0))
             def _():
-                send_block(s, 0, lax.rem(r + n_row - s, n_row), 0, blk)
-                send_block(slot1, 1, lax.rem(r + s, n_row), 0, blk)
-
-            @pl.when(last == 1)
+                send_half(s, 0, lax.rem(r + n_row - s, n_row), c0 // half)
+
+            @pl.when((last == 0) & (lax.rem(c0 + 1, half) == 0))
             def _():
-                send_block(far + far * (e - final), 0, lax.rem(r + far, n_row), (e - final) * hb, hb)
+                send_half(slot1, 1, lax.rem(r + s, n_row), c0 // half)
 
         @pl.when(e == attend_at)
         def _():
             prepare()
 
-        @pl.when((e >= attend_at) & (e < attend_at + 4))
-        def _():
-            lax.fori_loop((e - attend_at) * portion, (e - attend_at + 1) * portion, window, 0)
+        @pl.when((e >= attend_at) & (e < attend_at + 3))
+        def _():
+            begin = jnp.maximum(2 * pairs * (e - attend_at) - pairs // 2, 0) // 2
+            end = jnp.minimum(2 * pairs * (e - attend_at + 1) - pairs // 2, 2 * pairs) // 2
+            lax.fori_loop(begin, end, window, 0)
 
         @pl.when(e == events)
         def _():
             conclude()
+            for n, ref in ((1, aupd_ref), (2, tupd_ref)):
+                pltpu.make_async_copy(ref, outs[n], out_sems.at[n]).start()
 
         @pl.when(e == jnp.where(is_near, finish_at, events))
         def _():
@@ -452,6 +460,7 @@
 
     lax.fori_loop(0, events + 1, event, 0)
 
+    pltpu.make_async_copy(tri_ref, outs[0], out_sems.at[0]).start()
     for _ in range(2):
         wait_bytes(side_r.at[pl.ds(0, (n_col - 1) * blk)], sem_out.at[0])
     wait_bytes(mrecv.at[pl.ds(0, (n_col - 1) * blk)], m_send)
@@ -472,6 +481,8 @@
         wait_bytes(ring.at[0, c], ring_send.at[c % 2, far - 1, c])
     for copy in halos:
         copy.wait_send()
+    for n, ref in enumerate((tri_ref, aupd_ref, tupd_ref)):
+        pltpu.make_async_copy(ref, outs[n], out_sems.at[n]).wait()
 
 
 def attention(
@@ -585,8 +596,7 @@
     far = n_row // 2
     depth = n_col * cw
     blk = cpd * cw
-    vmem = pl.BlockSpec(memory_space=pltpu.VMEM)
-    smem = pl.BlockSpec(memory_space=pltpu.SMEM)
+    hbm = pl.BlockSpec(memory_space=pl.ANY)
     dma = pltpu.SemaphoreType.DMA
     rows = rt * cw
     wide = -(-3 * rt // LANES) * LANES
@@ -603,7 +613,7 @@
         pltpu.VMEM((cpd, depth, LANES), BF16),
         pltpu.VMEM((2 * far, cpd, rt, depth), BF16),
         pltpu.VMEM((2, sub * blk, LANES), F32),
-        pltpu.VMEM((2 * far + 1, sub * blk, LANES), BF16),
+        pltpu.VMEM((2 * far, sub * blk, LANES), BF16),
         pltpu.VMEM((LANES * cw, LANES), BF16),
         pltpu.VMEM((LANES * cw, LANES), F32),
         pltpu.VMEM((cw, rt, LANES), F32),
@@ -634,23 +644,34 @@
         dma((2, 2)),
         dma((2, 2)),
     ]
+    given = [
+        pair_act.reshape(rows, channels), pair_gain.reshape(1, -1), left_proj, right_proj, gate_proj, mix_gain.reshape(1, -1),
+        out_proj, bias_proj.T, token_single, cond_proj, atom_act.reshape(slots, channels), atom_gain.reshape(1, -1), qkv_proj,
+        attn_proj, token_proj, atom_token.reshape(-1, LANES), atom_mask.reshape(-1, LANES), key_start,
+    ]
+    held = [pltpu.VMEM(a.shape, a.dtype) for a in given[:-1]] + [pltpu.SMEM(given[-1].shape, given[-1].dtype)]
+    held += [pltpu.VMEM((rows, channels), BF16), pltpu.VMEM((slots, channels), BF16), pltpu.VMEM((rt, token_proj.shape[1]), BF16)]
+    held += [dma((len(given),)), dma((3,))]
+    n_in = len(given)
+
+    def unpack(*refs):
+        ins, outs, refs = refs[:n_in], refs[n_in : n_in + 3], refs[n_in + 3 :]
+        here, results, sems, rest = refs[:n_in], refs[n_in : n_in + 3], refs[n_in + 3 : n_in + 5], refs[n_in + 5 :]
+        kernel(n_row, n_col, rt, cw, ins, outs, here, *sems, *results, *rest)
+
     made = pl.pallas_call(
-        functools.partial(kernel, n_row, n_col, rt, cw),
+        unpack,
         out_shape=[
             jax.ShapeDtypeStruct((rows, channels), BF16),
             jax.ShapeDtypeStruct((slots, channels), BF16),
             jax.ShapeDtypeStruct((rt, token_proj.shape[1]), BF16),
         ],
-        in_specs=[vmem] * 17 + [smem],
-        out_specs=[vmem] * 3,
-        scratch_shapes=scratch,
+        in_specs=[hbm] * len(given),
+        out_specs=[hbm] * 3,
+        scratch_shapes=held + scratch,
         compiler_params=pltpu.CompilerParams(collective_id=0, has_side_effects=True, vmem_limit_bytes=56 * 1024 * 1024),
         name="triangle_attention",
-    )(
-        pair_act.reshape(rows, channels), pair_gain.reshape(1, -1), left_proj, right_proj, gate_proj, mix_gain.reshape(1, -1),
-        out_proj, bias_proj.T, token_single, cond_proj, atom_act.reshape(slots, channels), atom_gain.reshape(1, -1), qkv_proj,
-        attn_proj, token_proj, atom_token.reshape(-1, LANES), atom_mask.reshape(-1, LANES), key_start,
-    )
+    )(*given)
     tri, aupd, tupd = pl.pallas_call(
         hand_over,
         out_shape=[jax.ShapeDtypeStruct(a.shape, a.dtype) for a in made],

time: 88.4 us -> 84.2 us (0.952); the launches traced: 87.1 us -> 84.1 us
  Pallas kernels: 86.4 us -> 83.5 us
    pallas_call x1, Pallas kernels: 84.4 us -> 81.4 us  [body(): pl.pallas_call(unpack, out_shape=[jax.ShapeDtypeStruct((rows, channels),...]
where the time goes in v4:
time: 84.2 us; the launch traced here: 84.1 us
  Pallas kernels  83.5 us (99%)
    pallas_call x1, Pallas kernels, body(): pl.pallas_call(unpack, out_shape=[jax.ShapeDtypeStruct((rows, channels),...  81.4 us
    pallas_call x1, Pallas kernels, body(): pl.pallas_call(hand_over, out_shape=[jax.ShapeDtypeStruct(a.shape, a.dtyp...  2.01 us

profile of v4, /device:TPU:17, one launch (start us, length us, event | category | flops | bytes accessed | tf_op | source)
XLA Modules:
  0.0 84.1 jit_solution(8935769196941850641)
XLA Ops:
  0.6 81.4 %triangle_attention.1 = (bf16[2304,128]{1,0:T(8,128)(2,1)}, bf16[512,128]{1,0:T(8,128)(2,1)}, bf16[96,768]{1,0:T(8,128)(2,1)}) custom-call(bf16[2304,128]{1,0:T(8,128)(2,1)} %bitcast.11, f32[1,128]{1,0:T(1,128)} %bitcast.16, bf16[128,256]{1,0:T(8,128)(2,1)} %refs_2_.1, bf16[128,256]{1,0:T(8,128)(2,1)} %refs_3_.1, bf16[128,128]{1,0:T(8,128)(2,1)} %refs_4_.1, ...), custom_call_target="tpu_custom_call" | custom-call | tf_op jit(solution)/shard_map/triangle_attention/pallas_call | solution.py:662
  82.1 2.0 %hand_over.1 = (bf16[2304,128]{1,0:T(8,128)(2,1)}, bf16[512,128]{1,0:T(8,128)(2,1)}, bf16[96,768]{1,0:T(8,128)(2,1)}) custom-call(bf16[2304,128]{1,0:T(8,128)(2,1)} %get-tuple-element.9.a_ref, bf16[512,128]{1,0:T(8,128)(2,1)} %get-tuple-element.10.b_ref, bf16[96,768]{1,0:T(8,128)(2,1)} %get-tuple-element.11.c_ref), custom_call_target="tpu_custom_call" | custom-call | tf_op jit(solution)/shard_map/hand_over/pallas_call | solution.py:675

commit v5 on v4

--- a/solution.py
+++ b/solution.py
@@ -93,6 +93,7 @@
     sem_out,
     ring_send,
     ring_recv,
+    ring_tail,
     m_send,
     m_recv,
     b_send,
@@ -219,6 +220,9 @@
         pair = src[h, pl.ds(pl.multiple_of(p * 2 * hb, 16), 2 * hb), :].astype(F32)
         return jnp.concatenate([pair[c * cw : (c + 1) * cw], pair[hb + c * cw : hb + (c + 1) * cw]], axis=0)
 
+    sub_order = list(range(0, sub, 2)) + list(range(1, sub, 2))
+    piece = rt // 2
+
     for h in range(2):
         wait_bytes(recv_r.at[h], sem_r.at[h])
         for cc in range(half):
@@ -230,7 +234,9 @@
 
             lax.fori_loop(0, n_col // 2, gather_step, 0, unroll=4)
             for b in range(n_col * cw // LANES):
-                ring[0, c, :, b * LANES : (b + 1) * LANES] = rtr[b * LANES : (b + 1) * LANES, :].T[:rt].astype(BF16)
+                block = rtr[b * LANES : (b + 1) * LANES, :].T
+                block = jnp.concatenate([block[k * cw : (k + 1) * cw] for k in sub_order], axis=0)
+                ring[0, c, :, b * LANES : (b + 1) * LANES] = block.astype(BF16)
             to_row(right, ring.at[0, c], ring.at[1, c], ring_send.at[0, 0, c], ring_recv.at[0, 1, c]).start()
             to_row(left, ring.at[0, c], ring.at[far + 1, c], ring_send.at[1, 0, c], ring_recv.at[1, 1, c]).start()
 
@@ -281,11 +287,17 @@
 
     def multiply(slot, c, d):
         m = dot(ring[slot, c], lt[c])
-        for s in range(sub):
-            mf[d, pl.ds(pl.multiple_of((s * cpd + c) * cw, 8), cw), :] = m[s * cw : (s + 1) * cw]
-
-    def send_half(slot, d, source, h):
-        def step(s, _):
+        for k, s in enumerate(sub_order):
+            mf[d, pl.ds(pl.multiple_of((s * cpd + c) * cw, 8), cw), :] = m[k * cw : (k + 1) * cw]
+
+    def multiply_piece(slot, c, part):
+        m = dot(ring[slot, c, part * piece : (part + 1) * piece, :], lt[c])
+        for k, s in enumerate(range(part, sub, 2)):
+            mf[0, pl.ds(pl.multiple_of((s * cpd + c) * cw, 8), cw), :] = m[k * cw : (k + 1) * cw]
+
+    def send_half(slot, d, source, h, first=0, stride=1):
+        def step(n, _):
+            s = first + n * stride
             target = source * sub + s
             rows = pl.ds(pl.multiple_of(s * blk + h * hb, 16), hb)
             msend[slot, rows, :] = mf[d, rows, :].astype(BF16)
@@ -302,7 +314,7 @@
 
             return 0
 
-        lax.fori_loop(0, sub, step, 0)
+        lax.fori_loop(0, sub // stride, step, 0)
 
     owner = q // sub
     near = lax.rem(owner - r + 1 + n_row, n_row)
@@ -311,7 +323,7 @@
     events = final + half
     early = 3
     finish_at = cpd + 2
-    attend_at = final - 1
+    attend_at = final
     pairs = slots // QWIN // 2
 
     def place(e):
@@ -323,24 +335,21 @@
 
     def pass_on(e):
         s, c0, c1, slot1, last = place(e)
-        wait_bytes(ring.at[s, c0], ring_recv.at[0, s, c0])
         before = (s + 1) // far
-
-        @pl.when((last == 0) & (before * lax.rem(c0, 2) == 0))
-        def _():
-            to_row(right, ring.at[s, c0], ring.at[s + 1, c0], ring_send.at[0, s, c0], ring_recv.at[0, s + 1, c0]).start()
-
-        wait_bytes(ring.at[slot1, c1], ring_recv.at[1, s, c1])
-
-        @pl.when((last == 0) & (before * lax.rem(c0 + 1, 2) == 0))
-        def _():
-            to_row(
-                left,
-                ring.at[slot1, c1],
-                ring.at[s + 1 + far * (1 - before), c1],
-                ring_send.at[1, s, c1],
-                ring_recv.at[1, s + 1, c1],
-            ).start()
+        for direction, slot, target in ((0, s, right), (1, slot1, left)):
+            wait_bytes(ring.at[slot, c0], ring_recv.at[direction, s, c0])
+            src = ring.at[slot, c0]
+            sent = ring_send.at[direction, s, c0]
+
+            @pl.when(before == 0)
+            def _():
+                to_row(target, src, ring.at[slot + 1, c0], sent, ring_recv.at[direction, s + 1, c0]).start()
+
+            @pl.when((before == 1) & (lax.rem(c0 + direction, 2) == 0))
+            def _():
+                for part in range(2):
+                    rows = pl.ds(part * piece, piece)
+                    to_row(target, src.at[rows], ring.at[far, c0, rows], sent, ring_tail.at[part, c0]).start()
 
     def finish():
         wait_bytes(mrecv, m_recv)
@@ -418,32 +427,39 @@
     send_half(0, 0, r, 1)
 
     def event(e, _):
-        @pl.when((e >= early) & (e < events))
+        @pl.when((e >= early) & (e < final))
         def _():
             pass_on(e)
 
-        @pl.when(e < events)
+        @pl.when(e < final)
         def _():
             s, c0, c1, slot1, last = place(e)
             multiply(s, c0, 0)
-            multiply(slot1, c1, 1 - last)
-
-            @pl.when((last == 1) | (lax.rem(c0 + 1, half) == 0))
+            multiply(slot1, c1, 1)
+
+            @pl.when(lax.rem(c0 + 1, half) == 0)
             def _():
                 send_half(s, 0, lax.rem(r + n_row - s, n_row), c0 // half)
-
-            @pl.when((last == 0) & (lax.rem(c0 + 1, half) == 0))
-            def _():
                 send_half(slot1, 1, lax.rem(r + s, n_row), c0 // half)
 
+        @pl.when((e >= final) & (e < events))
+        def _():
+            s, c0, c1, slot1, last = place(e)
+            for part in range(2):
+                rows = pl.ds(part * piece, piece)
+                for c in (c0, c1):
+                    wait_bytes(ring.at[far, c, rows], ring_tail.at[part, c])
+                    multiply_piece(far, c, part)
+                send_half(far, 0, lax.rem(r + far, n_row), c0 // half, part, 2)
+
         @pl.when(e == attend_at)
         def _():
             prepare()
 
-        @pl.when((e >= attend_at) & (e < attend_at + 3))
-        def _():
-            begin = jnp.maximum(2 * pairs * (e - attend_at) - pairs // 2, 0) // 2
-            end = jnp.minimum(2 * pairs * (e - attend_at + 1) - pairs // 2, 2 * pairs) // 2
+        @pl.when((e >= attend_at) & (e < attend_at + 2))
+        def _():
+            begin = (e - attend_at) * pairs // 4
+            end = (e - attend_at + 1) * pairs // 4
             lax.fori_loop(begin, end, window, 0)
 
         @pl.when(e == events)
@@ -562,13 +578,21 @@
 
     def in_pairs(work):
         def step(p, _):
-            work(2 * p)
-            work(2 * p + 1)
+            for k in range(2):
+                work(2 * p + k)
             return 0
 
         return step
 
-    return in_pairs(ahead), prepare, in_pairs(window), conclude
+    def in_fours(work):
+        def step(p, _):
+            for k in range(4):
+                work(4 * p + k)
+            return 0
+
+        return step
+
+    return in_pairs(ahead), prepare, in_fours(window), conclude
 
 
 def hand_over(a_ref, b_ref, c_ref, a_out, b_out, c_out, ins, outs, a_mid, b_mid, c_mid):
@@ -636,7 +660,8 @@
         dma((2,)),
         dma((1,)),
         dma((2, far, cpd)),
-        dma((2, far + 1, cpd)),
+        dma((2, far, cpd)),
+        dma((2, cpd)),
         dma,
         dma,
         dma,

time: 84.2 us -> 80.9 us (0.961)
  Pallas kernels: 83.5 us -> 79.7 us
    pallas_call x1, Pallas kernels: 81.4 us -> 77.7 us  [body(): pl.pallas_call(unpack, out_shape=[jax.ShapeDtypeStruct((rows, channels),...]
where the time goes in v5:
time: 80.9 us; the launch traced here: 80.4 us
  Pallas kernels  79.7 us (99%)
    pallas_call x1, Pallas kernels, body(): pl.pallas_call(unpack, out_shape=[jax.ShapeDtypeStruct((rows, channels),...  77.7 us
    pallas_call x1, Pallas kernels, body(): pl.pallas_call(hand_over, out_shape=[jax.ShapeDtypeStruct(a.shape, a.dtyp...  2.01 us

profile of v5, /device:TPU:17, one launch (start us, length us, event | category | flops | bytes accessed | tf_op | source)
XLA Modules:
  0.0 80.4 jit_solution(3777844129599951208)
XLA Ops:
  0.6 77.7 %triangle_attention.1 = (bf16[2304,128]{1,0:T(8,128)(2,1)}, bf16[512,128]{1,0:T(8,128)(2,1)}, bf16[96,768]{1,0:T(8,128)(2,1)}) custom-call(bf16[2304,128]{1,0:T(8,128)(2,1)} %bitcast.11, f32[1,128]{1,0:T(1,128)} %bitcast.16, bf16[128,256]{1,0:T(8,128)(2,1)} %refs_2_.1, bf16[128,256]{1,0:T(8,128)(2,1)} %refs_3_.1, bf16[128,128]{1,0:T(8,128)(2,1)} %refs_4_.1, ...), custom_call_target="tpu_custom_call" | custom-call | tf_op jit(solution)/shard_map/triangle_attention/pallas_call | solution.py:687
  78.3 2.0 %hand_over.1 = (bf16[2304,128]{1,0:T(8,128)(2,1)}, bf16[512,128]{1,0:T(8,128)(2,1)}, bf16[96,768]{1,0:T(8,128)(2,1)}) custom-call(bf16[2304,128]{1,0:T(8,128)(2,1)} %get-tuple-element.9.a_ref, bf16[512,128]{1,0:T(8,128)(2,1)} %get-tuple-element.10.b_ref, bf16[96,768]{1,0:T(8,128)(2,1)} %get-tuple-element.11.c_ref), custom_call_target="tpu_custom_call" | custom-call | tf_op jit(solution)/shard_map/hand_over/pallas_call | solution.py:700

commit v6 on v5

--- a/solution.py
+++ b/solution.py
@@ -369,17 +369,17 @@
             trif[pl.ds(j, rt, stride=cw), :] = (gate[j] * projected).astype(BF16).astype(F32)
             return 0
 
-        lax.fori_loop(0, cw, step, 0, unroll=8)
+        lax.fori_loop(0, cw, step, 0, unroll=12)
 
         @pl.when(is_near)
         def _():
             def bias_step(j, _):
                 updated = (xf[pl.ds(j, rt, stride=cw), :] + trif[pl.ds(j, rt, stride=cw), :]).astype(BF16)
-                biasf[pl.ds(j, HEADS, stride=cw), :] = dot(bpt[...], padded(updated), NT)[:HEADS]
+                biasf[pl.ds(j, 8, stride=cw), :] = dot(bpt[...], padded(updated), NT)
                 return 0
 
             lax.fori_loop(0, cw, bias_step, 0, unroll=8)
-            bias_out[...] = biasf[...].astype(BF16)
+            bias_out[...] = biasf[: HEADS * cw, :].astype(BF16)
             dst = bias_in.at[pl.ds(pl.multiple_of((near * sub + lax.rem(q, sub)) * HEADS * cw, 16), HEADS * cw)]
 
             def share(d, _):
@@ -642,7 +642,7 @@
         pltpu.VMEM((LANES * cw, LANES), F32),
         pltpu.VMEM((cw, rt, LANES), F32),
         pltpu.VMEM((rows, LANES), F32),
-        pltpu.VMEM((HEADS * cw, LANES), F32),
+        pltpu.VMEM((8 * cw, LANES), F32),
         pltpu.VMEM((HEADS * cw, LANES), BF16),
         pltpu.VMEM((3 * sub * HEADS * cw, LANES), BF16),
         pltpu.VMEM((HEADS * wide, LANES), BF16),

time: 80.9 us -> 80.5 us (level)
  no operation moved by 1% of the time
where the time goes in v6:
time: 80.5 us; the launch traced here: 80.1 us
  Pallas kernels  79.5 us (99%)
    pallas_call x1, Pallas kernels, body(): pl.pallas_call(unpack, out_shape=[jax.ShapeDtypeStruct((rows, channels),...  77.5 us
    pallas_call x1, Pallas kernels, body(): pl.pallas_call(hand_over, out_shape=[jax.ShapeDtypeStruct(a.shape, a.dtyp...  2.01 us

profile of v6, /device:TPU:17, one launch (start us, length us, event | category | flops | bytes accessed | tf_op | source)
XLA Modules:
  0.0 80.1 jit_solution(3592280441468331678)
XLA Ops:
  0.6 77.5 %triangle_attention.1 = (bf16[2304,128]{1,0:T(8,128)(2,1)}, bf16[512,128]{1,0:T(8,128)(2,1)}, bf16[96,768]{1,0:T(8,128)(2,1)}) custom-call(bf16[2304,128]{1,0:T(8,128)(2,1)} %bitcast.11, f32[1,128]{1,0:T(1,128)} %bitcast.16, bf16[128,256]{1,0:T(8,128)(2,1)} %refs_2_.1, bf16[128,256]{1,0:T(8,128)(2,1)} %refs_3_.1, bf16[128,128]{1,0:T(8,128)(2,1)} %refs_4_.1, ...), custom_call_target="tpu_custom_call" | custom-call | tf_op jit(solution)/shard_map/triangle_attention/pallas_call | solution.py:687
  78.1 2.0 %hand_over.1 = (bf16[2304,128]{1,0:T(8,128)(2,1)}, bf16[512,128]{1,0:T(8,128)(2,1)}, bf16[96,768]{1,0:T(8,128)(2,1)}) custom-call(bf16[2304,128]{1,0:T(8,128)(2,1)} %get-tuple-element.9.a_ref, bf16[512,128]{1,0:T(8,128)(2,1)} %get-tuple-element.10.b_ref, bf16[96,768]{1,0:T(8,128)(2,1)} %get-tuple-element.11.c_ref), custom_call_target="tpu_custom_call" | custom-call | tf_op jit(solution)/shard_map/hand_over/pallas_call | solution.py:700

commit v7 on v6

--- a/solution.py
+++ b/solution.py
@@ -392,6 +392,7 @@
         def narrow(t, _):
             rows = pl.ds(pl.multiple_of(t * 384, 384), 384)
             tri_ref[rows, :] = trif[rows, :].astype(BF16)
+            pltpu.make_async_copy(tri_ref.at[rows], outs[0].at[rows], out_sems.at[0]).start()
             return 0
 
         lax.fori_loop(0, rt * cw // 384, narrow, 0, unroll=2)
@@ -476,7 +477,6 @@
 
     lax.fori_loop(0, events + 1, event, 0)
 
-    pltpu.make_async_copy(tri_ref, outs[0], out_sems.at[0]).start()
     for _ in range(2):
         wait_bytes(side_r.at[pl.ds(0, (n_col - 1) * blk)], sem_out.at[0])
     wait_bytes(mrecv.at[pl.ds(0, (n_col - 1) * blk)], m_send)

time: 80.5 us -> 80.5 us (level)
  no operation moved by 1% of the time
where the time goes in v7:
time: 80.5 us; the launch traced here: 80.1 us
  Pallas kernels  79.4 us (99%)
    pallas_call x1, Pallas kernels, body(): pl.pallas_call(unpack, out_shape=[jax.ShapeDtypeStruct((rows, channels),...  77.4 us
    pallas_call x1, Pallas kernels, body(): pl.pallas_call(hand_over, out_shape=[jax.ShapeDtypeStruct(a.shape, a.dtyp...  2.01 us

profile of v7, /device:TPU:17, one launch (start us, length us, event | category | flops | bytes accessed | tf_op | source)
XLA Modules:
  0.0 80.1 jit_solution(9006188577793311542)
XLA Ops:
  0.6 77.4 %triangle_attention.1 = (bf16[2304,128]{1,0:T(8,128)(2,1)}, bf16[512,128]{1,0:T(8,128)(2,1)}, bf16[96,768]{1,0:T(8,128)(2,1)}) custom-call(bf16[2304,128]{1,0:T(8,128)(2,1)} %bitcast.11, f32[1,128]{1,0:T(1,128)} %bitcast.16, bf16[128,256]{1,0:T(8,128)(2,1)} %refs_2_.1, bf16[128,256]{1,0:T(8,128)(2,1)} %refs_3_.1, bf16[128,128]{1,0:T(8,128)(2,1)} %refs_4_.1, ...), custom_call_target="tpu_custom_call" | custom-call | tf_op jit(solution)/shard_map/triangle_attention/pallas_call | solution.py:687
  78.1 2.0 %hand_over.1 = (bf16[2304,128]{1,0:T(8,128)(2,1)}, bf16[512,128]{1,0:T(8,128)(2,1)}, bf16[96,768]{1,0:T(8,128)(2,1)}) custom-call(bf16[2304,128]{1,0:T(8,128)(2,1)} %get-tuple-element.9.a_ref, bf16[512,128]{1,0:T(8,128)(2,1)} %get-tuple-element.10.b_ref, bf16[96,768]{1,0:T(8,128)(2,1)} %get-tuple-element.11.c_ref), custom_call_target="tpu_custom_call" | custom-call | tf_op jit(solution)/shard_map/hand_over/pallas_call | solution.py:700
